TPU v7x, 128 devices: a whole 4x4x4 slice. The times are simulated.
128 devices in a mesh: lon: 32 (over y, x_hi, z), lat: 4 (over x_lo, core).
Axes of the slice: x: 4 (x_hi: 2, x_lo: 2; x = x_hi * 2 + x_lo), y: 4, z: 4, core: 2. Of those that a mesh axis runs over, the one named last changes fastest.
Arguments:
- field: bfloat16 [8, 24, 73728], P(None, 'lat', 'lon'), may hold values from -6 to 6
- cotangent: bfloat16 [8, 24, 73728], P(None, 'lat', 'lon'), may hold values from -6 to 6
- gain_attn: float32 [192], replicated, may hold values from 0.25 to 1.75
- gain_mlp: float32 [192], replicated, may hold values from 0.25 to 1.75
- qkv_weight: bfloat16 [192, 576], replicated, may hold values from -0.4375 to 0.4375
- proj_weight: bfloat16 [192, 192], replicated, may hold values from -0.4375 to 0.4375
- fc1_weight: bfloat16 [192, 768], replicated, may hold values from -0.4375 to 0.4375
- fc2_weight: bfloat16 [768, 192], replicated, may hold values from -0.21875 to 0.21875
- bias_table: float32 [4, 4, 6, 23, 144], P(None, 'lat'), may hold values from -5 to 400
Outputs:
- mixed: bfloat16 [8, 24, 73728], P(None, 'lat', 'lon')
- field_grad: bfloat16 [8, 24, 73728], P(None, 'lat', 'lon')
- qkv_grad: float32 [192, 576], replicated
- proj_grad: float32 [192, 192], replicated
- fc1_grad: float32 [192, 768], replicated
- fc2_grad: float32 [768, 192], replicated
- gain_attn_grad: float32 [192], replicated
- gain_mlp_grad: float32 [192], replicated
- table_grad: float32 [4, 4, 6, 23, 144], P(None, 'lat')
All inputs are finite; a program needn't handle non-finite values.
Results may differ from a plain program's by a relative error of at most 0.034.
Values may be sent and summed in bfloat16 or wider, within the bound.
A program may use at most 192 MiB of HBM per device.

v0:
```python
import jax
import jax.numpy as jnp
from jax import lax
from jax.sharding import PartitionSpec as P

WIN_Z = 2
WIN_LAT = 6
WIN_LON = 12


EPSILON = 1e-05
MASKED = -1000000000.0


def shifted_2(value, axis, by):
    size = lax.axis_size(axis)
    return lax.ppermute(value, axis, [(i, (i + by) % size) for i in range(size)])


def product_of(form, left, right):
    return jnp.einsum(form, left, right, preferred_element_type=jnp.float32)


def norm_scale(values, gain):
    centre = values - jnp.mean(values, axis=-1, keepdims=True)
    spread = jnp.mean(centre * centre, axis=-1, keepdims=True)
    return centre * lax.rsqrt(spread + EPSILON) * gain


def gelu_tanh(values):
    return jax.nn.gelu(values, approximate=True)


def lead_roll(tile, channels):
    col_cut = WIN_LON // 2 * channels
    row_cut = WIN_LAT // 2
    ahead = shifted_2(tile[:, :, :col_cut], "lon", -1)
    moved = jnp.concatenate([tile[:, :, col_cut:], ahead], axis=2)
    below = shifted_2(moved[:, :row_cut], "lat", -1)
    moved = jnp.concatenate([moved[:, row_cut:], below], axis=1)
    return jnp.roll(moved, -1, axis=0)


def trail_roll(tile, channels):
    col_cut = WIN_LON // 2 * channels
    row_cut = WIN_LAT // 2
    moved = jnp.roll(tile, 1, axis=0)
    above = shifted_2(moved[:, -row_cut:], "lat", 1)
    moved = jnp.concatenate([above, moved[:, :-row_cut]], axis=1)
    behind = shifted_2(moved[:, :, -col_cut:], "lon", 1)
    return jnp.concatenate([behind, moved[:, :, :-col_cut]], axis=2)


def to_windows(tile, channels):
    level_count, row_count, flat = tile.shape
    col_count = flat // channels
    shaped = tile.reshape(
        level_count // WIN_Z,
        WIN_Z,
        row_count // WIN_LAT,
        WIN_LAT,
        col_count // WIN_LON,
        WIN_LON,
        channels,
    )
    shaped = shaped.transpose(0, 2, 4, 1, 3, 5, 6)
    return shaped.reshape(
        level_count // WIN_Z,
        row_count // WIN_LAT,
        col_count // WIN_LON,
        WIN_Z * WIN_LAT * WIN_LON,
        channels,
    )


def from_windows(windows):
    z_windows, a_windows, l_windows, tokens_win, channels = windows.shape
    shaped = windows.reshape(z_windows, a_windows, l_windows, WIN_Z, WIN_LAT, WIN_LON, channels)
    shaped = shaped.transpose(0, 3, 1, 4, 2, 5, 6)
    return shaped.reshape(z_windows * WIN_Z, a_windows * WIN_LAT, l_windows * WIN_LON * channels)


def regions(z_windows, a_windows, first_window, total_windows):
    level_in = jnp.arange(WIN_Z)[None, None, :, None, None]
    row_in = jnp.arange(WIN_LAT)[None, None, None, :, None]
    level_last = (jnp.arange(z_windows) == z_windows - 1)[:, None, None, None, None]
    row_last = (jnp.arange(a_windows) + first_window == total_windows - 1)[
        None, :, None, None, None
    ]
    level_label = jnp.logical_and(level_last, level_in == WIN_Z - 1).astype(jnp.int32)
    row_label = jnp.logical_and(row_last, row_in >= WIN_LAT - WIN_LAT // 2).astype(jnp.int32)
    labels = jnp.broadcast_to(
        2 * level_label + row_label, (z_windows, a_windows, WIN_Z, WIN_LAT, WIN_LON)
    )
    return labels.reshape(z_windows, a_windows, WIN_Z * WIN_LAT * WIN_LON)


def offset_table(rel_count):
    places = jnp.arange(WIN_LON)
    distance = places[:, None] - places[None, :] + WIN_LON - 1
    onehot = (distance[None, :, :] == jnp.arange(rel_count)[:, None, None]).astype(jnp.float32)
    return onehot.reshape(rel_count, WIN_LON * WIN_LON)


def expand_bias(table, labels):
    z_windows, a_windows, head_count, rel_count, pair_count = table.shape
    tokens_win = WIN_Z * WIN_LAT * WIN_LON
    spread = jnp.einsum(
        "abhrm,rn->abhmn", table, offset_table(rel_count), precision=lax.Precision.HIGHEST
    )
    spread = spread.reshape(
        z_windows, a_windows, head_count, WIN_Z, WIN_Z, WIN_LAT, WIN_LAT, WIN_LON, WIN_LON
    )
    spread = spread.transpose(0, 1, 2, 3, 5, 7, 4, 6, 8).reshape(
        z_windows, a_windows, head_count, tokens_win, tokens_win
    )
    allowed = labels[:, :, None, :, None] == labels[:, :, None, None, :]
    return jnp.where(allowed, spread, MASKED)


def shrink_bias(d_bias, rel_count):
    z_windows, a_windows, head_count, tokens_win, tokens_other = d_bias.shape
    shaped = d_bias.reshape(
        z_windows, a_windows, head_count, WIN_Z, WIN_LAT, WIN_LON, WIN_Z, WIN_LAT, WIN_LON
    )
    shaped = shaped.transpose(0, 1, 2, 3, 6, 4, 7, 5, 8).reshape(
        z_windows, a_windows, head_count, WIN_Z * WIN_Z * WIN_LAT * WIN_LAT, WIN_LON * WIN_LON
    )
    return jnp.einsum(
        "abhmn,rn->abhrm", shaped, offset_table(rel_count), precision=lax.Precision.HIGHEST
    )


def attend(windows, qkv_weight, proj_weight, bias_full):
    z_windows, a_windows, l_windows, tokens_win, channels = windows.shape
    head_count = bias_full.shape[2]
    head_size = channels // head_count
    scaling = head_size ** (-0.5)
    projected = product_of("abltc,cd->abltd", windows, qkv_weight)
    projected = projected.reshape(
        z_windows, a_windows, l_windows, tokens_win, 3, head_count, head_size
    )
    queries = (projected[:, :, :, :, 0] * scaling).astype(jnp.bfloat16)
    key_part = projected[:, :, :, :, 1].astype(jnp.bfloat16)
    value_part = projected[:, :, :, :, 2].astype(jnp.bfloat16)
    scores = product_of("abltho,ablsho->ablhts", queries, key_part) + bias_full[:, :, None]
    row_top = jnp.max(scores, axis=-1, keepdims=True)
    raised = jnp.exp(scores - row_top)
    softmaxed = raised / jnp.sum(raised, axis=-1, keepdims=True)
    context = product_of(
        "ablhts,ablsho->abltho", softmaxed.astype(jnp.bfloat16), value_part
    ).astype(jnp.bfloat16)
    context = context.reshape(z_windows, a_windows, l_windows, tokens_win, channels)
    attended = product_of("abltc,cd->abltd", context, proj_weight).astype(jnp.bfloat16)
    return (attended, (queries, key_part, value_part, softmaxed, context))


def attend_back(windows, d_attended, saved, qkv_weight, proj_weight):
    queries, key_part, value_part, softmaxed, context = saved
    z_windows, a_windows, l_windows, tokens_win, channels = windows.shape
    head_count = queries.shape[4]
    head_size = queries.shape[5]
    scaling = head_size ** (-0.5)
    d_proj = product_of("abltc,abltd->cd", context, d_attended)
    d_context = product_of("abltd,cd->abltc", d_attended, proj_weight).astype(jnp.bfloat16)
    d_context = d_context.reshape(
        z_windows, a_windows, l_windows, tokens_win, head_count, head_size
    )
    d_probs = product_of("abltho,ablsho->ablhts", d_context, value_part)
    d_values = product_of("ablhts,abltho->ablsho", softmaxed.astype(jnp.bfloat16), d_context)
    d_scores = softmaxed * (d_probs - jnp.sum(d_probs * softmaxed, axis=-1, keepdims=True))
    d_bias = jnp.sum(d_scores, axis=2)
    d_low = d_scores.astype(jnp.bfloat16)
    d_queries = product_of("ablhts,ablsho->abltho", d_low, key_part) * scaling
    d_keys = product_of("ablhts,abltho->ablsho", d_low, queries)
    d_projected = jnp.stack([d_queries, d_keys, d_values], axis=4)
    d_projected = d_projected.reshape(
        z_windows, a_windows, l_windows, tokens_win, 3 * channels
    ).astype(jnp.bfloat16)
    d_qkv = product_of("abltc,abltd->cd", windows, d_projected)
    d_windows = product_of("abltd,cd->abltc", d_projected, qkv_weight).astype(jnp.bfloat16)
    return (d_windows, d_qkv, d_proj, d_bias)


def mlp_pass(field_wide, attn_back, cotangent, gain_mlp, fc1_weight, fc2_weight):
    channels = gain_mlp.shape[0]
    contract_rows = (((0,), (0,)), ((), ()))
    contract_cols = (((1,), (1,)), ((), ()))
    resid = field_wide + attn_back.astype(jnp.float32)
    normed, norm_back = jax.vjp(norm_scale, resid, gain_mlp)
    normed_low = normed.astype(jnp.bfloat16).reshape(-1, channels)
    hidden_pre = jnp.dot(normed_low, fc1_weight, preferred_element_type=jnp.float32)
    activated, gelu_back = jax.vjp(gelu_tanh, hidden_pre)
    hidden_low = activated.astype(jnp.bfloat16)
    output = jnp.dot(hidden_low, fc2_weight, preferred_element_type=jnp.float32).reshape(
        resid.shape
    )
    mixed = (resid + output).astype(jnp.bfloat16)
    flat_cot = cotangent.reshape(-1, channels)
    d_fc2 = lax.dot_general(hidden_low, flat_cot, contract_rows, preferred_element_type=jnp.float32)
    d_hidden = lax.dot_general(
        flat_cot, fc2_weight, contract_cols, preferred_element_type=jnp.float32
    ).astype(jnp.bfloat16)
    d_pre = gelu_back(d_hidden.astype(jnp.float32))[0].astype(jnp.bfloat16)
    d_fc1 = lax.dot_general(normed_low, d_pre, contract_rows, preferred_element_type=jnp.float32)
    d_normed = lax.dot_general(
        d_pre, fc1_weight, contract_cols, preferred_element_type=jnp.float32
    ).reshape(resid.shape)
    d_resid_norm, d_gain_mlp = norm_back(d_normed)
    d_resid = cotangent.astype(jnp.float32) + d_resid_norm
    return (mixed, d_resid, d_fc1, d_fc2, d_gain_mlp)


def shards(
    field,
    cotangent,
    gain_attn,
    gain_mlp,
    qkv_weight,
    proj_weight,
    fc1_weight,
    fc2_weight,
    bias_table,
):
    channels = gain_attn.shape[0]
    level_count, row_count, flat = field.shape
    col_count = flat // channels
    grid_shape = (level_count, row_count, col_count, channels)
    tile_shape = (level_count, row_count, flat)
    z_windows = level_count // WIN_Z
    a_windows = row_count // WIN_LAT
    labels = regions(
        z_windows, a_windows, lax.axis_index("lat") * a_windows, a_windows * lax.axis_size("lat")
    )
    bias_full = expand_bias(bias_table, labels)
    field_wide = field.astype(jnp.float32).reshape(grid_shape)
    normed, norm_back = jax.vjp(norm_scale, field_wide, gain_attn)
    shifted = lead_roll(normed.astype(jnp.bfloat16).reshape(tile_shape), channels)
    windows = to_windows(shifted, channels)
    attended, saved = attend(windows, qkv_weight, proj_weight, bias_full)
    attn_back = trail_roll(from_windows(attended), channels)
    mixed, d_resid, d_fc1, d_fc2, d_gain_mlp = mlp_pass(
        field_wide,
        attn_back.reshape(grid_shape),
        cotangent.reshape(grid_shape),
        gain_mlp,
        fc1_weight,
        fc2_weight,
    )
    d_shifted_out = lead_roll(d_resid.astype(jnp.bfloat16).reshape(tile_shape), channels)
    d_windows, d_qkv, d_proj, d_bias = attend_back(
        windows, to_windows(d_shifted_out, channels), saved, qkv_weight, proj_weight
    )
    d_normed = trail_roll(from_windows(d_windows), channels)
    d_field_norm, d_gain_attn = norm_back(d_normed.reshape(grid_shape).astype(jnp.float32))
    field_grad = (d_resid + d_field_norm).astype(jnp.bfloat16).reshape(tile_shape)
    mixed_tile = mixed.reshape(tile_shape)
    d_table = shrink_bias(d_bias, bias_table.shape[3])
    qkv_sum, proj_sum, fc1_sum, fc2_sum, gain_attn_sum, gain_mlp_sum = lax.psum(
        (d_qkv, d_proj, d_fc1, d_fc2, d_gain_attn, d_gain_mlp), ("lon", "lat")
    )
    table_sum = lax.psum(d_table.astype(jnp.bfloat16), "lon").astype(jnp.float32)
    return (
        mixed_tile,
        field_grad,
        qkv_sum,
        proj_sum,
        fc1_sum,
        fc2_sum,
        gain_attn_sum,
        gain_mlp_sum,
        table_sum,
    )


def solution(mesh):
    return jax.shard_map(
        shards,
        mesh=mesh,
        in_specs=(
            P(None, "lat", "lon"),
            P(None, "lat", "lon"),
            P(),
            P(),
            P(),
            P(),
            P(),
            P(),
            P(None, "lat", None, None, None),
        ),
        out_specs=(
            P(None, "lat", "lon"),
            P(None, "lat", "lon"),
            P(),
            P(),
            P(),
            P(),
            P(),
            P(),
            P(None, "lat", None, None, None),
        ),
        check_vma=False,
    )
```

profile of v0, /device:TPU:1, one launch (start us, length us, event | category | flops | bytes accessed | tf_op | source)
XLA Modules:
  0.0 762.9 jit_solution(4078646827801764461)
XLA Ops:
  12.8 9.5 %collective-permute-start = (bf16[8,6,1152]{2,0,1:T(8,128)(2,1)}, bf16[8,6,1152]{2,0,1:T(8,128)(2,1)}, u32[]{:S(2)}, u32[]{:S(2)}) collective-permute-start(bf16[8,6,1152]{2,0,1:T(8,128)(2,1)} %get-tuple-element.71), channel_id=1, source_target_pairs={{0,124},{4,0},{8,4},{12,8},{16,12},{20,16},{24,20},{28,24},{32,28}... | collective-permute-start | bytes 331784 | tf_op jit(solution)/shard_map/ppermute | solution.py:17
  25.0 15.2 %convolution_bitcast_fusion = f32[4,1,6,2,6,12,2,6,12]{8,7,4,6,3,2,0,5,1:T(8,128)} fusion(f32[4,6,2,2,6,6,23]{6,0,5,4,3,2,1:T(4,128)S(1)} %bitcast.150, s32[12,12]{1,0:T(8,128)S(1)} %subtract_add_fusion), kind=kOutput, calls=%fused_computation.1 | convolution fusion | flops 137358576 | bytes 2309184 | tf_op jit(solution)/shard_map/abhrm,rn->abhmn/dot_general | solution.py:108
  44.7 39.3 %copy.173 = f32[4,1,6,2,6,12,2,6,12]{5,4,3,8,7,6,2,0,1:T(8,128)} copy(f32[4,1,6,2,6,12,2,6,12]{8,7,4,6,3,2,0,5,1:T(8,128)} %convolution_bitcast_fusion) | data formatting | bytes 3981312 | tf_op jit(solution)/shard_map/reshape | solution.py:114
  83.9 19.5 %reshape.500 = f32[4,6,144,144]{2,3,1,0:T(8,128)} reshape(f32[4,1,6,2,6,12,2,6,12]{5,4,3,8,7,6,2,0,1:T(8,128)} %copy.173) | data formatting | bytes 3981312 | tf_op jit(solution)/shard_map/reshape | solution.py:114
  108.7 2.8 fusion.68
  111.5 4.8 convolution_convert_fusion.1
  123.9 6.9 collective-permute-done.3
  154.1 2.2 sub.115
  157.5 2.1 mul.273
  160.9 2.2 reshape.481
  163.1 3.2 fusion.60
  169.9 4.2 collective-permute-start.5
  178.5 4.8 convolution_bitcast_fusion.2
  183.3 2.9 multiply_reduce_fusion
  187.1 2.4 convolution_bitcast_fusion.3
  193.3 5.6 copy.158
  199.9 18.5 %reshape.486 = f32[4,1,6,2,6,12,2,6,12]{8,7,6,5,4,3,2,0,1:T(8,128)} reshape(f32[4,6,144,144]{3,2,1,0:T(8,128)} %copy.158) | data formatting | bytes 3981312 | tf_op jit(solution)/shard_map/reshape | solution.py:123
  218.4 25.5 %copy.159 = f32[4,1,6,2,2,6,6,12,12]{8,7,6,5,4,3,2,0,1:T(8,128)} copy(f32[4,1,6,2,2,6,6,12,12]{8,6,4,7,5,3,2,0,1:T(8,128)} %bitcast.147) | data formatting | bytes 3981312 | tf_op jit(solution)/shard_map/transpose | solution.py:126
  243.9 19.5 %reshape.487 = f32[4,6,144,144]{3,2,1,0:T(8,128)} reshape(f32[4,1,6,2,2,6,6,12,12]{8,7,6,5,4,3,2,0,1:T(8,128)} %copy.159) | data formatting | bytes 3981312 | tf_op jit(solution)/shard_map/reshape.93
  263.4 4.5 fusion.14
  272.5 305.8 %all-reduce.5.cloned.1.call-done = bf16[4,1,6,23,144]{4,3,2,0,1:T(8,128)(2,1)} async-done(((bf16[4,1,6,23,144]{4,3,2,0,1:T(8,128)(2,1)}), bf16[4,1,6,23,144]{4,3,2,0,1:T(8,128)(2,1)}) %all-reduce.5.cloned.1.call-update) | async-done | bytes 158992 | tf_op jit(solution)/shard_map/psum | solution.py:262
  578.3 2.2 copy.160
  584.2 78.5 %all-reduce = (f32[192]{0:T(256)}, f32[192]{0:T(256)}) all-reduce(f32[192]{0:T(256)S(1)} %reduce_sum.158, f32[192]{0:T(256)S(1)} %copy-done.50), channel_id=1, replica_groups=mesh['lon'=32,'lat'=4] {'lon','lat'}, use_global_device_ids=true, to_apply=%region_17.18 | all-reduce | flops 384 | bytes 3072 | tf_op jit(solution)/shard_map/psum | solution.py:259
  662.7 88.0 %all-reduce.7.cloned.1.call-done = (f32[192,576]{1,0:T(8,128)}, f32[192,192]{1,0:T(8,128)}, f32[192,768]{1,0:T(8,128)}, f32[768,192]{0,1:T(8,128)}) async-done(((f32[192,576]{1,0:T(8,128)}, f32[192,192]{1,0:T(8,128)}, f32[192,768]{1,0:T(8,128)}, f32[768,192]{0,1:T(8,128)}), (f32[192,576]{1,0:T(8,128)}, f32[192,192]{1,0:T(8,128)}, f32[192,768]{1,0:T(8,128)}, ...) | async-done | bytes 1769488 | tf_op jit(solution)/shard_map/psum | solution.py:259
  (245 shorter events, 77.8 us)
Async XLA Ops:
  7.2 131.1 %copy-start = (bf16[192,768]{1,0:T(8,128)(2,1)S(1)}, bf16[192,768]{1,0:T(8,128)(2,1)}, u32[]{:S(2)}) copy-start(bf16[192,768]{1,0:T(8,128)(2,1)} %param.15) | copy-start | bytes 884740
  7.2 571.1 %all-reduce.5.cloned.1.call-start = ((), (), s32[]{:S(2)}) async-start(), calls=%async_computation | async-start | bytes 589824 | tf_op jit(solution)/shard_map/psum | solution.py:262
  12.0 11.2 %copy-start.10 = (f32[8,6,2304]{2,0,1:T(8,128)}, f32[8,6,2304]{2,0,1:T(8,128)S(1)}, u32[]{:S(2)}) copy-start(f32[8,6,2304]{2,0,1:T(8,128)S(1)} %sub.100) | copy-start | bytes 1327108
  12.0 10.3 %copy-start.32 = (f32[4,1,6,23,144]{4,1,3,2,0:T(1,128)S(1)}, f32[4,1,6,23,144]{4,1,3,2,0:T(1,128)}, u32[]{:S(2)}) copy-start(f32[4,1,6,23,144]{4,1,3,2,0:T(1,128)} %param.17) | copy-start | bytes 953860
  12.8 27.7 %collective-permute-start = (bf16[8,6,1152]{2,0,1:T(8,128)(2,1)}, bf16[8,6,1152]{2,0,1:T(8,128)(2,1)}, u32[]{:S(2)}, u32[]{:S(2)}) collective-permute-start(bf16[8,6,1152]{2,0,1:T(8,128)(2,1)} %get-tuple-element.71), channel_id=1, source_target_pairs={{0,124},{4,0},{8,4},{12,8},{16,12},{20,16},{24,20},{28,24},{32,28}... | collective-permute-start | bytes 331784 | tf_op jit(solution)/shard_map/ppermute | solution.py:17
  41.4 62.0 %collective-permute-start.1 = (bf16[8,3,2304]{2,0,1:T(8,128)(2,1)S(1)}, bf16[8,3,2304]{2,0,1:T(8,128)(2,1)S(1)}, u32[]{:S(2)}, u32[]{:S(2)}) collective-permute-start(bf16[8,3,2304]{2,0,1:T(8,128)(2,1)S(1)} %get-tuple-element.69), channel_id=1, source_target_pairs={{0,3},{1,0},{2,1},{3,2},{4,7},{5,4},{6,5},{7,6},{8,11},{9,8},{10,9... | collective-permute-start | bytes 331784 | tf_op jit(solution)/shard_map/ppermute | solution.py:17
  106.4 5.1 copy-start.15
  118.2 2.6 collective-permute-start.2
  120.9 13.2 %copy-start.17 = (bf16[8,6,1152]{2,0,1:T(8,128)(2,1)}, bf16[8,6,1152]{2,0,1:T(8,128)(2,1)S(1)}, u32[]{:S(2)}) copy-start(bf16[8,6,1152]{2,0,1:T(8,128)(2,1)S(1)} %get-tuple-element.67) | copy-start | bytes 331780
  120.9 9.9 %collective-permute-start.3 = (bf16[8,6,1152]{2,0,1:T(8,128)(2,1)S(1)}, bf16[8,6,1152]{2,0,1:T(8,128)(2,1)S(1)}, u32[]{:S(2)}, u32[]{:S(2)}) collective-permute-start(bf16[8,6,1152]{2,0,1:T(8,128)(2,1)S(1)} %get-tuple-element.66), channel_id=1, source_target_pairs={{0,4},{4,8},{8,12},{12,16},{16,20},{20,24},{24,28},{28,32},{32,36}... | collective-permute-start | bytes 331784 | tf_op jit(solution)/shard_map/ppermute | solution.py:17
  154.1 5.5 copy-start.12
  154.1 5.5 copy-start.38
  166.2 7.9 %copy-start.21 = (bf16[576,192]{1,0:T(8,128)(2,1)S(1)}, bf16[576,192]{1,0:T(8,128)(2,1)}, u32[]{:S(2)}) copy-start(bf16[576,192]{1,0:T(8,128)(2,1)} %reshape_reshape.3) | copy-start | bytes 663556
  166.2 3.7 collective-permute-start.4
  169.9 8.0 %copy-start.36 = (bf16[192,192]{1,0:T(8,128)(2,1)S(1)}, bf16[192,192]{1,0:T(8,128)(2,1)}, u32[]{:S(2)}) copy-start(bf16[192,192]{1,0:T(8,128)(2,1)} %param.14) | copy-start | bytes 221188
  169.9 7.4 collective-permute-start.5
  178.5 4.8 copy-start.16
  193.3 5.6 copy-start.43
  199.7 69.7 %collective-permute-start.6 = (bf16[8,3,2304]{2,0,1:T(8,128)(2,1)}, bf16[8,3,2304]{2,0,1:T(8,128)(2,1)}, u32[]{:S(2)}, u32[]{:S(2)}) collective-permute-start(bf16[8,3,2304]{2,0,1:T(8,128)(2,1)} %fusion.40), channel_id=1, source_target_pairs={{0,1},{1,2},{2,3},{3,0},{4,5},{5,6},{6,7},{7,4},{8,9},{9,10},{10,1... | collective-permute-start | bytes 331784 | tf_op jit(solution)/shard_map/ppermute | solution.py:17
  267.9 482.7 %all-reduce.7.cloned.1.call-start = ((), (), s32[]{:S(2)}) async-start(), calls=%async_computation.1 | async-start | bytes 3735552 | tf_op jit(solution)/shard_map/psum | solution.py:259
  270.4 310.1 %copy-start.25 = (bf16[8,6,1152]{2,0,1:T(8,128)(2,1)}, bf16[8,6,1152]{2,0,1:T(8,128)(2,1)S(1)}, u32[]{:S(2)}) copy-start(bf16[8,6,1152]{2,0,1:T(8,128)(2,1)S(1)} %get-tuple-element.61) | copy-start | bytes 331780
  270.4 310.1 %collective-permute-start.7 = (bf16[8,6,1152]{2,0,1:T(8,128)(2,1)S(1)}, bf16[8,6,1152]{2,0,1:T(8,128)(2,1)S(1)}, u32[]{:S(2)}, u32[]{:S(2)}) collective-permute-start(bf16[8,6,1152]{2,0,1:T(8,128)(2,1)S(1)} %get-tuple-element.60), channel_id=1, source_target_pairs={{0,4},{4,8},{8,12},{12,16},{16,20},{20,24},{24,28},{28,32},{32,36}... | collective-permute-start | bytes 331784 | tf_op jit(solution)/shard_map/ppermute | solution.py:17
  272.4 308.4 %copy-start.49 = (f32[192]{0:T(256)S(1)}, f32[192]{0:T(256)}, u32[]{:S(2)}) copy-start(f32[192]{0:T(256)} %param.11) | copy-start | bytes 2308
  750.6 5.2 copy-start.1
  (37 other events, 83.8 us)
Sparse Core Ops, SparseCore 0:
  268.0 310.1 all-reduce.4
  585.2 165.3 all-reduce.6
where the time goes:
time: 770 us; the launch traced here: 763 us
  waiting for transfers between devices  406 us (53%)
  local copies, waits for them, and re-layouts  175 us (23%)
  blocking collectives  78.5 us (10%)
  matrix products  50.9 us (7%)
  other arithmetic  19.7 us (3%)
  starting transfers between devices  17.2 us (2%)
  between operations  15.2 us (2%)
    psum x1, waiting for transfers between devices, shards(): lax.psum(d_table.astype(jnp.bfloat16), 'lon').astype(jnp.float32)  306 us
    psum x1, waiting for transfers between devices, shards(): lax.psum((d_qkv, d_proj, d_fc1, d_fc2, d_gain_attn, d_gain_mlp), ('lon',...  88 us
    psum x1, blocking collectives, shards(): lax.psum((d_qkv, d_proj, d_fc1, d_fc2, d_gain_attn, d_gain_mlp), ('lon',...  78.5 us
    reshape x2, local copies, waits for them, and re-layouts, expand_bias(): spread.transpose(0, 1, 2, 3, 5, 7, 4, 6, 8)  58.8 us
    transpose x1, local copies, waits for them, and re-layouts, shrink_bias(): shaped.transpose(0, 1, 2, 3, 6, 4, 7, 5, 8)  25.5 us
    dot_general x12, matrix products, product_of(): return jnp.einsum(form, left, right, preferred_element_type=jnp.float32)  23.1 us
    another operation x4, local copies, waits for them, and re-layouts  22.1 us
    reshape x1, local copies, waits for them, and re-layouts, shrink_bias(): d_bias.reshape(z_windows, a_windows, head_count, WIN_Z, WIN_LAT, WIN_LON,...  18.5 us
  transfers between devices with their start and end apart: 10, of which 6 were waited for; matrix products, arithmetic and copies ran while one was open for 21% of the time, Pallas kernels for 0%

commit v1 on v0

v1 whole, which is shorter than its diff:
```python
import functools
import jax
import jax.numpy as jnp
import numpy as np
from jax import lax
from jax.experimental import pallas as pl
from jax.experimental.pallas import tpu as pltpu
from jax.sharding import PartitionSpec as P

BF = jnp.bfloat16
F32 = jnp.float32
C = 192
HEADS = 6
HEAD = 32
HID = 768
WZ, WR, WC = 2, 6, 12
A = WZ * WR
TW = A * WC
NW = 4
TOK = NW * TW
REL = 2 * WC - 1
RELP = 24
HT = HEADS * TW
ZL = REL * HEADS * A
EPS = 1e-05
MASKED = -1000000000.0


def constants():
    perm = np.zeros((WC, 8, 8, NW, WC, WZ, WR), np.float32)
    for c in range(WC):
        for w in range(NW):
            for lev in range(WZ):
                for r in range(WR):
                    perm[c, (2 * w + lev + 1) % 8, r, w, c, lev, r] = 1
    perm = perm.reshape(WC * 64, TOK)
    expand = np.zeros((WC, A, WC, HEADS, A), np.float32)
    for c in range(WC):
        for a in range(A):
            expand[c, a, c, :, a] = 1
    expand = expand.reshape(TW, HT)
    head_mask = np.zeros((HEADS, HEAD, WC, HEADS, A), np.float32)
    for h in range(HEADS):
        head_mask[h, :, :, h, :] = 1
    head_mask = head_mask.reshape(C, HT)
    rep = np.zeros((HEADS, RELP, REL, HEADS, A), np.float32)
    for h in range(HEADS):
        for rel in range(REL):
            rep[h, rel, rel, h, :] = 1
    rep = rep.reshape(HEADS * RELP, ZL)
    pair = np.zeros((WZ, WZ, WR, WR, WZ, WR, 16), np.float32)
    for lt in range(WZ):
        for ls in range(WZ):
            for rt in range(WR):
                for rs in range(WR):
                    pair[lt, ls, rt, rs, lt, rt, ls * WR + rs] = 1
    pair = pair.reshape(TW, A * 16)
    lane_a = np.arange(ZL) % A
    entry = (np.arange(A)[:, None] == lane_a[None, :]).astype(np.float32)
    entry = np.concatenate([entry, np.zeros((4, ZL), np.float32)])
    b = np.arange(16)
    level_differs = ((b[:, None] // WR) != (lane_a[None, :] // WR)) & (b[:, None] < A)
    row_differs = ((b[:, None] % WR >= 3) != (lane_a[None, :] % WR >= 3)) & (b[:, None] < A)
    differs = np.stack([level_differs, row_differs]).astype(np.float32)
    return [np.asarray(v, dtype=BF) for v in (perm, expand, head_mask, rep, pair)] + [entry, differs]


def nn(a, b):
    return lax.dot_general(a, b, (((1,), (0,)), ((), ())), preferred_element_type=F32)


def nt(a, b):
    return lax.dot_general(a, b, (((1,), (1,)), ((), ())), preferred_element_type=F32)


def tn(a, b):
    return lax.dot_general(a, b, (((0,), (0,)), ((), ())), preferred_element_type=F32)


def column_of(row):
    size = row.shape[1]
    eye = lax.broadcasted_iota(jnp.int32, (size, size), 0) == lax.broadcasted_iota(jnp.int32, (size, size), 1)
    return jnp.sum(jnp.where(eye, row, 0.0), axis=1, keepdims=True)


def row_of(column):
    size = column.shape[0]
    eye = lax.broadcasted_iota(jnp.int32, (size, size), 0) == lax.broadcasted_iota(jnp.int32, (size, size), 1)
    return jnp.sum(jnp.where(eye, column, 0.0), axis=0, keepdims=True)


def normalise(v):
    centre = v - jnp.sum(v, axis=0, keepdims=True) * (1.0 / C)
    inv = lax.rsqrt(jnp.sum(centre * centre, axis=0, keepdims=True) * (1.0 / C) + EPS)
    return centre * inv, inv


def normalise_back(g, hat, inv):
    return inv * (g - jnp.sum(g, axis=0, keepdims=True) * (1.0 / C) - hat * (jnp.sum(g * hat, axis=0, keepdims=True) * (1.0 / C)))


def gather_tokens(x_ref, own, lon, lat, diag):
    for c in range(WC):
        at = slice(c % 6 * C, (c % 6 + 1) * C)
        top, low = (own, lat) if c < 6 else (lon, diag)
        x_ref[c, :, 0:3, :] = top[:, :, at].astype(F32)[:, 3:6, :]
        x_ref[c, :, 3:6, :] = low[:, :, at].astype(F32)[:, 0:3, :]


HALF = WC * C // 2
LANES = 128
PEERS = 16
ROWS = (80, 32)
TROWS = 48
MESH_ID = pl.DeviceIdType.MESH


def place():
    lon, lat = lax.axis_index("lon"), lax.axis_index("lat")
    z, xh, y = lon % 4, (lon // 4) % 2, lon // 8
    return lon, lat, y * 4 + z, xh, xh * 2 + lat // 2, lat % 2


def plane_id(p, xh, lat):
    return ((p // 4) * 8 + xh * 4 + p % 4, lat)


def column_id(t, me, core):
    return ((me // 4) * 8 + (t // 2) * 4 + me % 4, (t % 2) * 2 + core)


def remote(src, dst, sends, recvs, k, device):
    return pltpu.make_async_remote_copy(
        src_ref=src, dst_ref=dst, send_sem=sends.at[k], recv_sem=recvs.at[k], device_id=device, device_id_type=MESH_ID
    )


def total(ref, count):
    value = ref[0].astype(F32)
    for k in range(1, count):
        value = value + ref[k].astype(F32)
    return value.astype(BF)


class PlaneSum:
    def __init__(self, piece, terms, part, cross, final, plane_sems, x_sems, back_sems, local_sem, table):
        self.piece, self.terms, self.part, self.cross, self.final = piece, terms, part, cross, final
        self.plane_sems, self.x_sems, self.back_sems, self.local_sem, self.table = plane_sems, x_sems, back_sems, local_sem, table
        self.lon, self.lat, self.me, self.xh, self.xi, self.core = place()

    def start(self):
        self.copies = []
        for s in range(1, PEERS):
            p = (self.me + s) % PEERS
            copy = remote(self.piece(p), self.terms.at[s], *self.plane_sems, s, plane_id(p, self.xh, self.lat))
            copy.start()
            self.copies.append(copy)

    def across(self):
        self.terms[0] = self.piece(self.me)[...]
        for copy in self.copies:
            copy.wait()
        value = total(self.terms, PEERS)
        self.part[...] = value
        count = 2 if self.table else 4
        mine = self.xh if self.table else self.xi
        self.cross[mine] = value
        self.copies = []
        for s in range(1, count):
            t = (mine + s) % count
            device = ((self.me // 4) * 8 + t * 4 + self.me % 4, self.lat) if self.table else column_id(t, self.me, self.core)
            copy = remote(self.part, self.cross.at[mine], *self.x_sems, s, device)
            copy.start()
            self.copies.append(copy)

    def back(self):
        for copy in self.copies:
            copy.wait()
        self.part[...] = total(self.cross, 2 if self.table else 4)
        self.own = pltpu.make_async_copy(self.part, self.final(self.me), self.local_sem)
        self.own.start()
        self.copies = []
        for s in range(1, PEERS):
            p = (self.me + s) % PEERS
            copy = remote(self.part, self.final(self.me), *self.back_sems, s, plane_id(p, self.xh, self.lat))
            copy.start()
            self.copies.append(copy)

    def finish(self):
        self.own.wait()
        for copy in self.copies:
            copy.wait()


class CoreSum(PlaneSum):
    def __init__(self, grads, got, halves, final, core_sems, rows, *args):
        self.grads, self.got, self.halves, self.whole, self.core_sems, self.rows = grads, got, halves, final, core_sems, rows
        core = lax.axis_index("lat") % 2
        super().__init__(lambda p: halves.at[p], args[0], args[1], args[2], lambda p: final.at[core * PEERS + p], *args[3:], False)

    def start_core(self):
        other = (self.lon, self.lat // 2 * 2 + 1 - self.core)
        self.swap = remote(self.grads.at[pl.ds((1 - self.core) * PEERS, PEERS)], self.got, *self.core_sems, 0, other)
        self.swap.start()

    def start(self):
        self.swap.wait()
        for p in range(PEERS):
            self.halves[p] = (self.grads[self.core * PEERS + p].astype(F32) + self.got[p].astype(F32)).astype(BF)
        super().start()

    def finish(self):
        super().finish()
        other = (self.lon, self.lat // 2 * 2 + 1 - self.core)
        mine = self.whole.at[pl.ds(self.core * PEERS, PEERS)]
        self.swap = remote(mine, mine, *self.core_sems, 1, other)
        self.swap.start()

    def finish_core(self):
        self.swap.wait()


def put_tiles(ref, rows, first, value):
    done = 0
    while done < value.shape[0]:
        piece, row = divmod(first + done, rows)
        count = min(rows - row, value.shape[0] - done)
        ref[piece, row:row + count, :] = value[done:done + count]
        done += count


def get_tiles(ref, rows, first, count):
    parts, done = [], 0
    while done < count:
        piece, row = divmod(first + done, rows)
        take = min(rows - row, count - done)
        parts.append(ref[piece, row:row + take, :].astype(F32))
        done += take
    return parts[0] if len(parts) == 1 else jnp.concatenate(parts, axis=0)


def block_kernel(
    field_ref, cot_ref, gain_attn, gain_mlp, qkv_w, proj_w, fc1_w, fc2_w, table,
    perm, expand, head_mask, rep, pair, entry, differs,
    mixed_own, mixed_got, fgrad_own, fgrad_got, final0, final1, final_t,
    x_ref, t_ref, bias_ref, z_ref, p_ref, qblk_ref, q_ref, k_ref, v_ref, kv_ref, ctx_ref, dctx_ref, dproj_ref,
    halo_ref, send_ref, grads0, grads1, grads_t, got0, got1, halves0, halves1,
    terms0, terms1, terms_t, part0, part1, part_t, cross0, cross1, cross_t,
    local_sems, halo_send, halo_recv, trail_send, trail_recv, core_send, core_recv,
    plane_send, plane_recv, x_send, x_recv, back_send, back_recv,
):
    lon, lat, me, xh, xi, core = place()
    lon_n, lat_n = 32, 4
    west, east = (lon + lon_n - 1) % lon_n, (lon + 1) % lon_n
    above, below = (lat + lat_n - 1) % lat_n, (lat + 1) % lat_n

    barrier = pltpu.get_barrier_semaphore()
    partners = [(west, lat), (east, lat), (lon, above), (lon, below), (west, above), (east, below)]
    partners += [(lon, lat // 2 * 2 + 1 - core)]
    partners += [plane_id((me + s) % PEERS, xh, lat) for s in range(1, PEERS)]
    partners += [column_id((xi + s) % 4, me, core) for s in range(1, 4)]
    for device in partners:
        pl.semaphore_signal(barrier, inc=1, device_id=device, device_id_type=MESH_ID)
    pl.semaphore_wait(barrier, len(partners))

    halos = []
    for k, source in enumerate((field_ref, cot_ref)):
        first, last = source.at[:, :, pl.ds(0, HALF)], source.at[:, :, pl.ds(HALF, HALF)]
        own = pltpu.make_async_copy(last, halo_ref.at[4 * k], local_sems.at[k])
        copies = [own]
        for s, (piece, device) in enumerate(((first, (west, lat)), (last, (lon, above)), (first, (west, above)))):
            copies.append(remote(piece, halo_ref.at[4 * k + 1 + s], halo_send, halo_recv, 3 * k + s, device))
        for copy in copies:
            copy.start()
        halos.append(copies)

    def trail(value, k, own, got):
        for c in range(WC):
            rows = value[c * 64:(c + 1) * 64].astype(F32).reshape(8, 8, C)[:, 0:6, :].astype(BF)
            send_ref[2 * k + c // 6, :, :, c % 6 * C:(c % 6 + 1) * C] = rows
        first, last = send_ref.at[2 * k], send_ref.at[2 * k + 1]
        copies = [pltpu.make_async_copy(first, own, local_sems.at[2 + k])]
        for s, (piece, device) in enumerate(((last, (east, lat)), (first, (lon, below)), (last, (east, below)))):
            copies.append(remote(piece, got.at[s], trail_send, trail_recv, 3 * k + s, device))
        for copy in copies:
            copy.start()
        return copies

    sums = []
    for k, (grads, got, halves, final, terms, part, cross) in enumerate((
        (grads0, got0, halves0, final0, terms0, part0, cross0), (grads1, got1, halves1, final1, terms1, part1, cross1)
    )):
        sums.append(CoreSum(
            grads, got, halves, final, (core_send.at[k], core_recv.at[k]), ROWS[k], terms, part, cross,
            (plane_send.at[k], plane_recv.at[k]), (x_send.at[k], x_recv.at[k]), (back_send.at[k], back_recv.at[k]), local_sems.at[4 + k],
        ))
    sum0, sum1 = sums
    sum_t = PlaneSum(
        lambda p: grads_t.at[p], terms_t, part_t, cross_t, lambda p: final_t.at[p],
        (plane_send.at[2], plane_recv.at[2]), (x_send.at[2], x_recv.at[2]), (back_send.at[2], back_recv.at[2]), local_sems.at[6], True,
    )

    t_ref[...] = jnp.zeros_like(t_ref)
    for w in range(NW):
        for h in range(HEADS):
            t_ref[h * RELP:h * RELP + REL, :] = table[w, 0, h]
        left = t_ref[...]
        spread = None
        for part in range(3):
            low = left.astype(BF)
            left = left - low.astype(F32)
            moved = nn(low, pair[...]).astype(BF)
            term = tn(moved, rep[...])
            spread = term if spread is None else spread + term
        z = spread[0:16] * entry[0:1]
        for a in range(1, A):
            z = z + spread[16 * a:16 * a + 16] * entry[a:a + 1]
        hide = jnp.where(lat == lat_n - 1, differs[1], 0.0)
        if w == NW - 1:
            hide = hide + differs[0]
        z = jnp.where(hide > 0.5, MASKED, z)
        for cs in range(WC):
            bias_ref[w, cs * A:(cs + 1) * A, :] = z[0:A, (11 - cs) * HEADS * A:(11 - cs) * HEADS * A + HT]

    x_ref[...] = jnp.zeros_like(x_ref)
    for copy in halos[0]:
        copy.wait()
    gather_tokens(x_ref, halo_ref.at[0], halo_ref.at[1], halo_ref.at[2], halo_ref.at[3])
    field = tn(x_ref[...].reshape(WC * 64, C).astype(BF), perm[...])

    gain1 = column_of(gain_attn[...])
    gain2 = column_of(gain_mlp[...])
    hat1, inv1 = normalise(field)
    normed1 = (hat1 * gain1).astype(BF)
    projected = tn(qkv_w[...], normed1)
    scaling = HEAD ** (-0.5)
    q_ref[...] = (projected[0:C] * scaling).astype(BF)
    k_ref[...] = projected[C:2 * C].astype(BF)
    v_ref[...] = projected[2 * C:].astype(BF)
    kv_ref[...] = tn(normed1, qkv_w[:, C:]).astype(BF)
    mask = head_mask[...].astype(F32)

    for w in range(NW):
        rows = slice(w * TW, (w + 1) * TW)
        qblk = (nn(q_ref[:, rows], expand[...]) * mask).astype(BF)
        qblk_ref[w] = qblk
        scores = nn(kv_ref[rows, 0:C], qblk) + bias_ref[w]
        raised = jnp.exp(scores - jnp.max(scores, axis=0, keepdims=True))
        probs = raised * (1.0 / jnp.sum(raised, axis=0, keepdims=True))
        p_ref[w] = probs
        context = (nn(v_ref[:, rows], probs.astype(BF)) * mask).astype(BF)
        ctx_ref[:, rows] = nt(context, expand[...]).astype(BF)
    attended = tn(proj_w[...], ctx_ref[...]).astype(BF)

    for copy in halos[1]:
        copy.wait()
    gather_tokens(x_ref, halo_ref.at[4], halo_ref.at[5], halo_ref.at[6], halo_ref.at[7])
    cot = tn(x_ref[...].reshape(WC * 64, C).astype(BF), perm[...])
    cot_low = cot.astype(BF)

    resid = field + attended.astype(F32)
    hat2, inv2 = normalise(resid)
    normed2 = (hat2 * gain2).astype(BF)
    hidden = tn(fc1_w[...], normed2)
    k0 = 0.7978845608028654
    k1 = 0.044715
    sq = hidden * hidden
    th = jnp.tanh(hidden * (k0 + (k0 * k1) * sq))
    half = 0.5 * (1.0 + th)
    act = (hidden * half).astype(BF)
    slope = half + 0.5 * hidden * (1.0 - th * th) * (k0 + (3.0 * k0 * k1) * sq)
    d_act = nn(fc2_w[...], cot_low).astype(BF)
    d_pre = (d_act.astype(F32) * slope).astype(BF)
    fc1_grad = nt(normed2, d_pre).astype(BF)
    fc2_grad = nt(cot_low, act).astype(BF)
    for k in range(6):
        put_tiles(grads0, ROWS[0], k * C, fc1_grad[:, k * LANES:(k + 1) * LANES])
        put_tiles(grads0, ROWS[0], (6 + k) * C, fc2_grad[:, k * LANES:(k + 1) * LANES])
    d_normed2 = nn(fc1_w[...], d_pre)
    gain2_grad = row_of(jnp.sum(d_normed2 * hat2, axis=1, keepdims=True))
    d_resid = cot + normalise_back(d_normed2 * gain2, hat2, inv2)
    d_att = d_resid.astype(BF)
    proj_grad = nt(ctx_ref[...], d_att).astype(BF)
    put_tiles(grads0, ROWS[0], 12 * C, proj_grad[:, C - LANES:])
    gain_rows = jnp.concatenate([gain2_grad[:, 0:LANES], gain2_grad[:, C - LANES:], jnp.zeros((62, LANES), F32)], axis=0)
    put_tiles(grads0, ROWS[0], 13 * C, gain_rows.astype(BF))
    sum0.start_core()
    mixed = (resid + tn(fc2_w[...], act)).astype(BF)
    mixed_copies = trail(nt(perm[...], mixed).astype(BF), 0, mixed_own, mixed_got)
    dctx_ref[...] = nn(proj_w[...], d_att).astype(BF)

    for w in range(NW):
        if w == 1:
            sum0.start()
        if w == 3:
            sum0.across()
        rows = slice(w * TW, (w + 1) * TW)
        dblk = (nn(dctx_ref[:, rows], expand[...]) * mask).astype(BF)
        probs = p_ref[w]
        d_probs = nn(kv_ref[rows, C:], dblk)
        weighted = probs * d_probs
        d_scores = weighted - probs * jnp.sum(weighted, axis=0, keepdims=True)
        d_low = d_scores.astype(BF)
        dproj_ref[2 * C:, rows] = nt(dblk, probs.astype(BF)).astype(BF)
        dproj_ref[C:2 * C, rows] = nt(qblk_ref[w], d_low).astype(BF)
        d_q = (nn(k_ref[:, rows], d_low) * (mask * scaling)).astype(BF)
        dproj_ref[0:C, rows] = nt(d_q, expand[...]).astype(BF)
        z_ref[...] = jnp.zeros_like(z_ref)
        for cs in range(WC):
            at = slice((11 - cs) * HEADS * A, (11 - cs) * HEADS * A + HT)
            z_ref[0:A, at] += d_scores[cs * A:(cs + 1) * A]
        dz = z_ref[...]
        spread = jnp.concatenate([dz * entry[a:a + 1] for a in range(A)], axis=0).astype(BF)
        d_table = nt(nt(rep[...], spread).astype(BF), pair[...]).astype(BF)
        for k in range(3):
            grads_t[3 * w + k] = d_table[TROWS * k:TROWS * (k + 1), 0:LANES]
            grads_t[12 + k, :, 16 * w:16 * w + 16] = d_table[TROWS * k:TROWS * (k + 1), LANES:]
    zeros_t = jnp.zeros((TROWS, 64), BF)
    for k in range(3):
        grads_t[12 + k, :, 64:] = zeros_t
    grads_t[15] = jnp.zeros((TROWS, LANES), BF)
    sum_t.start()
    sum0.back()

    dproj = dproj_ref[...]
    qkv_grad = nt(normed1, dproj).astype(BF)
    d_win = nn(qkv_w[...], dproj).astype(BF).astype(F32)
    gain1_grad = row_of(jnp.sum(d_win * hat1, axis=1, keepdims=True))
    for k in range(4):
        put_tiles(grads1, ROWS[1], k * C, qkv_grad[:, k * LANES:(k + 1) * LANES])
    put_tiles(grads1, ROWS[1], 4 * C, jnp.concatenate([qkv_grad[:, 4 * LANES:], proj_grad[:, 0:64]], axis=1))
    gain_rows = jnp.concatenate([gain1_grad[:, 0:LANES], gain1_grad[:, C - LANES:], jnp.zeros((62, LANES), F32)], axis=0)
    put_tiles(grads1, ROWS[1], 5 * C, gain_rows.astype(BF))
    sum1.start_core()
    d_field = (d_resid + normalise_back(d_win * gain1, hat1, inv1)).astype(BF)
    fgrad_copies = trail(nt(perm[...], d_field).astype(BF), 1, fgrad_own, fgrad_got)
    sum1.start()
    sum_t.across()
    sum0.finish()
    sum1.across()
    sum_t.back()
    sum0.finish_core()
    sum1.back()
    sum_t.finish()
    sum1.finish()
    sum1.finish_core()
    for copy in mixed_copies + fgrad_copies:
        copy.wait()


def results_kernel(
    mixed_own, mixed_got, fgrad_own, fgrad_got, final0, final1, final_t,
    mixed, fgrad, qkv, proj, fc1, fc2, gain_attn, gain_mlp, table,
):
    for own, got, out in ((mixed_own, mixed_got, mixed), (fgrad_own, fgrad_got, fgrad)):
        for at, top, low in ((0, got.at[2], got.at[0]), (HALF, got.at[1], own)):
            rows = jnp.concatenate([top[...].astype(F32)[:, 3:6, :], low[...].astype(F32)[:, 0:3, :]], axis=1)
            out[:, :, at:at + HALF] = rows.astype(BF)
    for k in range(6):
        fc1[:, k * LANES:(k + 1) * LANES] = get_tiles(final0, ROWS[0], k * C, C)
        fc2[k * LANES:(k + 1) * LANES, :] = get_tiles(final0, ROWS[0], (6 + k) * C, C).T
    proj[:, 64:] = get_tiles(final0, ROWS[0], 12 * C, C)
    for k in range(4):
        qkv[:, k * LANES:(k + 1) * LANES] = get_tiles(final1, ROWS[1], k * C, C)
    shared = get_tiles(final1, ROWS[1], 4 * C, C)
    qkv[:, 4 * LANES:] = shared[:, 0:64]
    proj[:, 0:64] = shared[:, 64:]
    for out, final, row in ((gain_attn, final1, 5 * C), (gain_mlp, final0, 13 * C)):
        rows = get_tiles(final, final.shape[1], row, 16)
        out[:, 0:LANES] = rows[0:1]
        out[:, LANES:] = rows[1:2, 64:]
    for w in range(NW):
        wide = jnp.concatenate([final_t[3 * w + k].astype(F32) for k in range(3)], axis=0)
        tail = jnp.concatenate([final_t[12 + k].astype(F32) for k in range(3)], axis=0)
        for h in range(HEADS):
            table[w, 0, h, :, 0:LANES] = wide[h * RELP:h * RELP + REL]
            table[w, 0, h, :, LANES:] = tail[h * RELP:h * RELP + REL, 16 * w:16 * w + 16]


def shards(field, cotangent, gain_attn, gain_mlp, qkv_weight, proj_weight, fc1_weight, fc2_weight, bias_table):
    consts = [jnp.asarray(v) for v in constants()]
    sds = jax.ShapeDtypeStruct
    vm = pl.BlockSpec(memory_space=pltpu.VMEM)
    hbm = pl.BlockSpec(memory_space=pl.ANY)
    half = (8, 6, HALF)
    dma = pltpu.SemaphoreType.DMA
    pieces = pl.pallas_call(
        block_kernel,
        out_shape=(
            sds(half, BF), sds((3,) + half, BF), sds(half, BF), sds((3,) + half, BF),
            sds((2 * PEERS, ROWS[0], LANES), BF), sds((2 * PEERS, ROWS[1], LANES), BF), sds((PEERS, TROWS, LANES), BF),
        ),
        in_specs=[hbm] * 2 + [vm] * (7 + len(consts)),
        out_specs=(hbm,) * 7,
        scratch_shapes=[
            pltpu.VMEM((WC, 8, 8, C), F32),
            pltpu.VMEM((HEADS * RELP, TW), F32),
            pltpu.VMEM((NW, TW, HT), F32),
            pltpu.VMEM((16, ZL), F32),
            pltpu.VMEM((NW, TW, HT), F32),
            pltpu.VMEM((NW, C, HT), BF),
            pltpu.VMEM((C, TOK), BF), pltpu.VMEM((C, TOK), BF), pltpu.VMEM((C, TOK), BF),
            pltpu.VMEM((TOK, 2 * C), BF),
            pltpu.VMEM((C, TOK), BF), pltpu.VMEM((C, TOK), BF),
            pltpu.VMEM((3 * C, TOK), BF),
            pltpu.VMEM((8,) + half, BF),
            pltpu.VMEM((4,) + half, BF),
            pltpu.VMEM((2 * PEERS, ROWS[0], LANES), BF), pltpu.VMEM((2 * PEERS, ROWS[1], LANES), BF), pltpu.VMEM((PEERS, TROWS, LANES), BF),
            pltpu.VMEM((PEERS, ROWS[0], LANES), BF), pltpu.VMEM((PEERS, ROWS[1], LANES), BF),
            pltpu.VMEM((PEERS, ROWS[0], LANES), BF), pltpu.VMEM((PEERS, ROWS[1], LANES), BF),
            pltpu.VMEM((PEERS, ROWS[0], LANES), BF), pltpu.VMEM((PEERS, ROWS[1], LANES), BF), pltpu.VMEM((PEERS, TROWS, LANES), BF),
            pltpu.VMEM((ROWS[0], LANES), BF), pltpu.VMEM((ROWS[1], LANES), BF), pltpu.VMEM((TROWS, LANES), BF),
            pltpu.VMEM((4, ROWS[0], LANES), BF), pltpu.VMEM((4, ROWS[1], LANES), BF), pltpu.VMEM((2, TROWS, LANES), BF),
            dma((7,)), dma((6,)), dma((6,)), dma((6,)), dma((6,)), dma((2, 2)), dma((2, 2)),
            dma((3, PEERS)), dma((3, PEERS)), dma((3, 4)), dma((3, 4)), dma((3, PEERS)), dma((3, PEERS)),
        ],
        compiler_params=pltpu.CompilerParams(vmem_limit_bytes=56 * 1024 * 1024, collective_id=0, has_side_effects=True),
        name="block",
    )(field, cotangent, gain_attn.reshape(1, C), gain_mlp.reshape(1, C), qkv_weight, proj_weight, fc1_weight, fc2_weight, bias_table, *consts)
    tile = field.shape
    mixed, fgrad, qkv, proj, fc1, fc2, gain1, gain2, table = pl.pallas_call(
        results_kernel,
        out_shape=(
            sds(tile, BF), sds(tile, BF), sds((C, 3 * C), F32), sds((C, C), F32), sds((C, HID), F32), sds((HID, C), F32),
            sds((1, C), F32), sds((1, C), F32), sds(bias_table.shape, F32),
        ),
        in_specs=[vm] * 7,
        out_specs=(vm,) * 9,
        compiler_params=pltpu.CompilerParams(vmem_limit_bytes=32 * 1024 * 1024),
        name="results",
    )(*pieces)
    return mixed, fgrad, qkv, proj, fc1, fc2, gain1.reshape(C), gain2.reshape(C), table


def solution(mesh):
    grid = P(None, "lat", "lon")
    by_type = P(None, "lat", None, None, None)
    return jax.shard_map(
        shards,
        mesh=mesh,
        in_specs=(grid, grid) + (P(),) * 6 + (by_type,),
        out_specs=(grid, grid) + (P(),) * 6 + (by_type,),
        check_vma=False,
    )
```

time: 770 us -> 95.6 us (0.12)
  waiting for transfers between devices: 406 us -> 0 us
  local copies, waits for them, and re-layouts: 175 us -> 15 us
  Pallas kernels: 0 us -> 79.5 us
  blocking collectives: 78.5 us -> 0 us
  matrix products: 50.9 us -> 0 us
  other arithmetic: 19.7 us -> 0 us
  starting transfers between devices: 17.2 us -> 0 us
  between operations: 15.2 us -> 0.69 us
    psum x2 -> x0, waiting for transfers between devices: 394 us -> none  [the longest x1 306 us: shards(): lax.psum(d_table.astype(jnp.bfloat16), 'lon').astype(jnp.float32)]
    reshape x7 -> x0, local copies, waits for them, and re-layouts: 82.8 us -> none  [the longest x2 58.8 us: expand_bias(): spread.transpose(0, 1, 2, 3, 5, 7, 4, 6, 8)]
    pallas_call x0 -> x2, Pallas kernels: none -> 79.5 us  [the longest x1 78 us: shards(): pl.pallas_call(block_kernel, out_shape=(sds(half, BF), sds((3,) + half, B...]
    psum x1 -> x0, blocking collectives: 78.5 us -> none  [shards(): lax.psum((d_qkv, d_proj, d_fc1, d_fc2, d_gain_attn, d_gain_mlp), ('lon',...]
    dot_general x20 -> x0, matrix products: 50.9 us -> none  [the longest x12 23.1 us: product_of(): return jnp.einsum(form, left, right, preferred_element_type=jnp.float32)]
    transpose x1 -> x0, local copies, waits for them, and re-layouts: 25.5 us -> none  [shrink_bias(): shaped.transpose(0, 1, 2, 3, 6, 4, 7, 5, 8)]
    another operation x7 -> x0, local copies, waits for them, and re-layouts: 23.9 us -> none
    ppermute x8 -> x0, starting transfers between devices: 17.1 us -> none  [shifted_2(): lax.ppermute(value, axis, [(i, (i + by) % size) for i in range(size)])]
  transfers between devices with their start and end apart: 10 -> 0, of which waited for: 6 -> 0; matrix products, arithmetic and copies ran while one was open for 21% -> 0% of each run, Pallas kernels for 0% -> 0%
where the time goes in v1:
time: 95.6 us; the launch traced here: 95.3 us
  Pallas kernels  79.5 us (83%)
  local copies, waits for them, and re-layouts  15 us (16%)
    pallas_call x1, Pallas kernels, shards(): pl.pallas_call(block_kernel, out_shape=(sds(half, BF), sds((3,) + half, B...  78 us
    unnamed x28, local copies, waits for them, and re-layouts  15 us

profile of v1, /device:TPU:1, one launch (start us, length us, event | category | flops | bytes accessed | tf_op | source)
XLA Modules:
  0.0 95.3 jit_solution(1296357653822886217)
XLA Ops:
  0.6 0.0 copy-start.9
  0.7 0.0 copy-start.8
  0.7 1.8 %copy.25.field_ref = bf16[8,6,2304]{2,1,0:T(8,128)(2,1)} copy(bf16[8,6,2304]{2,0,1:T(8,128)(2,1)} %param.16) | data formatting | bytes 442368 | tf_op args[0]
  2.4 0.0 copy-done.9
  2.4 0.0 copy-start.7
  2.4 0.8 copy.26.cot_ref
  3.2 0.0 copy-done.8
  3.2 0.9 copy.27.fc2_w
  4.1 0.0 copy-done.7
  4.1 0.9 copy.28.table
  5.0 78.0 %block.1 = (bf16[8,6,1152]{2,1,0:T(8,128)(2,1)}, bf16[3,8,6,1152]{3,2,1,0:T(8,128)(2,1)}, bf16[8,6,1152]{2,1,0:T(8,128)(2,1)}, bf16[3,8,6,1152]{3,2,1,0:T(8,128)...) custom-call(bf16[8,6,2304]{2,1,0:T(8,128)(2,1)} %copy.25.field_ref, ...), custom_call_target="tpu_custom_call" | custom-call | tf_op jit(solution)/shard_map/block/pallas_call | solution.py:487
  83.0 0.0 copy-start
  83.0 1.1 %copy-done = bf16[32,80,128]{2,1,0:T(8,128)(2,1)S(1)} copy-done((bf16[32,80,128]{2,1,0:T(8,128)(2,1)S(1)}, bf16[32,80,128]{2,1,0:T(8,128)(2,1)}, u32[]{:S(2)}) %copy-start) | copy-done | bytes 655384
  84.1 1.0 %copy-done.1 = bf16[3,8,6,1152]{3,2,1,0:T(8,128)(2,1)S(1)} copy-done((bf16[3,8,6,1152]{3,2,1,0:T(8,128)(2,1)S(1)}, bf16[3,8,6,1152]{3,2,1,0:T(8,128)(2,1)}, u32[]{:S(2)}) %copy-start.1) | copy-done | bytes 331800
  85.1 1.0 %copy-done.2 = bf16[3,8,6,1152]{3,2,1,0:T(8,128)(2,1)S(1)} copy-done((bf16[3,8,6,1152]{3,2,1,0:T(8,128)(2,1)S(1)}, bf16[3,8,6,1152]{3,2,1,0:T(8,128)(2,1)}, u32[]{:S(2)}) %copy-start.2) | copy-done | bytes 331800
  86.1 0.9 copy-done.3
  87.1 0.9 copy-done.4
  88.0 0.9 copy-done.5
  88.9 0.9 copy-done.6
  89.8 1.5 %results.1 = (bf16[8,6,2304]{2,1,0:T(8,128)(2,1)S(1)}, bf16[8,6,2304]{2,1,0:T(8,128)(2,1)S(1)}, f32[192,576]{1,0:T(8,128)}, f32[192,192]{1,0:T(8,128)}, f32[192,...) custom-call(bf16[8,6,1152]{2,1,0:T(8,128)(2,1)S(1)} %copy-done.5, ...), custom_call_target="tpu_custom_call" | custom-call | tf_op jit(solution)/shard_map/results/pallas_call | solution.py:521
  91.4 0.7 copy.29
  92.1 0.7 copy.30
  92.8 1.4 %copy.32 = f32[4,1,6,23,144]{4,1,3,2,0:T(1,128)} copy(f32[4,1,6,23,144]{4,3,2,1,0:T(8,128)S(1)} %get-tuple-element.49) | data formatting | bytes 635904
  94.2 1.1 %copy.31 = f32[768,192]{0,1:T(8,128)} copy(f32[768,192]{1,0:T(8,128)S(1)} %get-tuple-element.46) | data formatting | bytes 1179648
  (6 shorter events, 0.0 us)
Async XLA Ops:
  0.6 1.8 %copy-start.9 = (bf16[8,6,2304]{2,0,1:T(8,128)(2,1)S(1)}, bf16[8,6,2304]{2,0,1:T(8,128)(2,1)}, u32[]{:S(2)}) copy-start(bf16[8,6,2304]{2,0,1:T(8,128)(2,1)} %param.17) | copy-start | bytes 663556
  0.7 2.5 %copy-start.8 = (bf16[768,192]{0,1:T(8,128)(2,1)S(1)}, bf16[768,192]{0,1:T(8,128)(2,1)}, u32[]{:S(2)}) copy-start(bf16[768,192]{0,1:T(8,128)(2,1)} %param.23) | copy-start | bytes 884740
  2.4 1.7 %copy-start.7 = (f32[4,1,6,23,144]{4,1,3,2,0:T(1,128)S(1)}, f32[4,1,6,23,144]{4,1,3,2,0:T(1,128)}, u32[]{:S(2)}) copy-start(f32[4,1,6,23,144]{4,1,3,2,0:T(1,128)} %param.24) | copy-start | bytes 953860
  83.0 1.1 %copy-start = (bf16[32,80,128]{2,1,0:T(8,128)(2,1)S(1)}, bf16[32,80,128]{2,1,0:T(8,128)(2,1)}, u32[]{:S(2)}) copy-start(bf16[32,80,128]{2,1,0:T(8,128)(2,1)} %get-tuple-element.29.final0) | copy-start | bytes 1966084
  84.1 1.0 %copy-start.1 = (bf16[3,8,6,1152]{3,2,1,0:T(8,128)(2,1)S(1)}, bf16[3,8,6,1152]{3,2,1,0:T(8,128)(2,1)}, u32[]{:S(2)}) copy-start(bf16[3,8,6,1152]{3,2,1,0:T(8,128)(2,1)} %get-tuple-element.26.mixed_got) | copy-start | bytes 995332
  85.1 1.0 %copy-start.2 = (bf16[3,8,6,1152]{3,2,1,0:T(8,128)(2,1)S(1)}, bf16[3,8,6,1152]{3,2,1,0:T(8,128)(2,1)}, u32[]{:S(2)}) copy-start(bf16[3,8,6,1152]{3,2,1,0:T(8,128)(2,1)} %get-tuple-element.28.fgrad_got) | copy-start | bytes 995332
  86.1 0.9 copy-start.3
  87.1 0.9 copy-start.4
  88.0 0.9 copy-start.5
  88.9 0.9 copy-start.6

commit v2 on v1

v2 whole, which is shorter than its diff:
```python
import functools
import jax
import jax.numpy as jnp
import numpy as np
from jax import lax
from jax.experimental import pallas as pl
from jax.experimental.pallas import tpu as pltpu
from jax.sharding import PartitionSpec as P

BF = jnp.bfloat16
F32 = jnp.float32
C = 192
HEADS = 6
HEAD = 32
HID = 768
WZ, WR, WC = 2, 6, 12
A = WZ * WR
TW = A * WC
NW = 4
TOK = NW * TW
REL = 2 * WC - 1
RELP = 24
HT = HEADS * TW
ZL = REL * HEADS * A
EPS = 1e-05
MASKED = -1000000000.0


def constants():
    perm = np.zeros((WC, WR, 8, NW, WC, WZ, WR), np.float32)
    for c in range(WC):
        for w in range(NW):
            for lev in range(WZ):
                for r in range(WR):
                    perm[c, r, (2 * w + lev + 1) % 8, w, c, lev, r] = 1
    perm = perm.reshape(TOK, TOK)
    expand = np.zeros((WC, A, WC, HEADS, A), np.float32)
    for c in range(WC):
        for a in range(A):
            expand[c, a, c, :, a] = 1
    expand = expand.reshape(TW, HT)
    head_mask = np.zeros((HEADS, HEAD, WC, HEADS, A), np.float32)
    for h in range(HEADS):
        head_mask[h, :, :, h, :] = 1
    head_mask = head_mask.reshape(C, HT)
    rep = np.zeros((HEADS, RELP, REL, HEADS, A), np.float32)
    for h in range(HEADS):
        for rel in range(REL):
            rep[h, rel, rel, h, :] = 1
    rep = rep.reshape(HEADS * RELP, ZL)
    pair = np.zeros((WZ, WZ, WR, WR, WZ, WR, 16), np.float32)
    for lt in range(WZ):
        for ls in range(WZ):
            for rt in range(WR):
                for rs in range(WR):
                    pair[lt, ls, rt, rs, lt, rt, ls * WR + rs] = 1
    pair = pair.reshape(TW, A * 16)
    lane_a = np.arange(ZL) % A
    entry = (np.arange(A)[:, None] == lane_a[None, :]).astype(np.float32)
    entry = np.concatenate([entry, np.zeros((4, ZL), np.float32)])
    b = np.arange(16)
    level_differs = ((b[:, None] // WR) != (lane_a[None, :] // WR)) & (b[:, None] < A)
    row_differs = ((b[:, None] % WR >= 3) != (lane_a[None, :] % WR >= 3)) & (b[:, None] < A)
    differs = np.stack([level_differs, row_differs]).astype(np.float32)
    return [np.asarray(v, dtype=BF) for v in (perm, expand, head_mask, rep, pair)] + [entry, differs]


def nn(a, b):
    return lax.dot_general(a, b, (((1,), (0,)), ((), ())), preferred_element_type=F32)


def nt(a, b):
    return lax.dot_general(a, b, (((1,), (1,)), ((), ())), preferred_element_type=F32)


def tn(a, b):
    return lax.dot_general(a, b, (((0,), (0,)), ((), ())), preferred_element_type=F32)


def column_of(row):
    size = row.shape[1]
    eye = lax.broadcasted_iota(jnp.int32, (size, size), 0) == lax.broadcasted_iota(jnp.int32, (size, size), 1)
    return jnp.sum(jnp.where(eye, row, 0.0), axis=1, keepdims=True)


def row_of(column):
    size = column.shape[0]
    eye = lax.broadcasted_iota(jnp.int32, (size, size), 0) == lax.broadcasted_iota(jnp.int32, (size, size), 1)
    return jnp.sum(jnp.where(eye, column, 0.0), axis=0, keepdims=True)


def normalise(v):
    centre = v - jnp.sum(v, axis=0, keepdims=True) * (1.0 / C)
    inv = lax.rsqrt(jnp.sum(centre * centre, axis=0, keepdims=True) * (1.0 / C) + EPS)
    return centre * inv, inv


def normalise_back(g, hat, inv):
    return inv * (g - jnp.sum(g, axis=0, keepdims=True) * (1.0 / C) - hat * (jnp.sum(g * hat, axis=0, keepdims=True) * (1.0 / C)))


def tokens_of(x_ref, win):
    for c in range(WC):
        x_ref[c * 48:(c + 1) * 48, :] = win[:, :, c * C:(c + 1) * C].astype(F32).reshape(48, C)
    return x_ref[...].astype(BF)


HALF = WC * C // 2
LANES = 128
PEERS = 16
ROWS = (80, 32)
TROWS = 48
MESH_ID = pl.DeviceIdType.MESH


def place():
    lon, lat = lax.axis_index("lon"), lax.axis_index("lat")
    return (lon // 4) % 2 * 2 + lat // 2, lon // 8, lon % 4, lat % 2


def device_at(x, y, z, core):
    return ((y * 2 + x // 2) * 4 + z, x % 2 * 2 + core)


def remote(src, dst, sends, recvs, k, device):
    return pltpu.make_async_remote_copy(
        src_ref=src, dst_ref=dst, send_sem=sends.at[k], recv_sem=recvs.at[k], device_id=device, device_id_type=MESH_ID
    )


def total(ref, count):
    value = ref[0].astype(F32)
    for k in range(1, count):
        value = value + ref[k].astype(F32)
    return value.astype(BF)


class PlaneSum:
    def __init__(self, axes, piece, terms, part, cross, final, plane_sems, x_sems, back_sems, local_sem):
        self.axes, self.piece, self.terms, self.part, self.cross, self.final = axes, piece, terms, part, cross, final
        self.plane_sems, self.x_sems, self.back_sems, self.local_sem = plane_sems, x_sems, back_sems, local_sem
        self.at = place()
        self.me = self.at[axes[0]] * 4 + self.at[axes[1]]
        self.count = cross.shape[0]
        self.step = 4 // self.count
        self.mine = self.at[axes[2]] // self.step

    def in_plane(self, s):
        p = (self.me + s) % PEERS
        at = list(self.at)
        at[self.axes[0]], at[self.axes[1]] = p // 4, p % 4
        return p, device_at(*at)

    def along(self, s):
        at = list(self.at)
        at[self.axes[2]] = (at[self.axes[2]] + s * self.step) % 4
        return device_at(*at)

    def partners(self):
        return [self.in_plane(s)[1] for s in range(1, PEERS)] + [self.along(s) for s in range(1, self.count)]

    def start(self):
        self.copies = []
        for s in range(1, PEERS):
            p, device = self.in_plane(s)
            copy = remote(self.piece(p), self.terms.at[s], *self.plane_sems, s, device)
            copy.start()
            self.copies.append(copy)

    def across(self):
        self.terms[0] = self.piece(self.me)[...]
        for copy in self.copies:
            copy.wait()
        value = total(self.terms, PEERS)
        self.part[...] = value
        self.cross[self.mine] = value
        self.copies = []
        for s in range(1, self.count):
            copy = remote(self.part, self.cross.at[self.mine], *self.x_sems, s, self.along(s))
            copy.start()
            self.copies.append(copy)

    def back(self):
        for copy in self.copies:
            copy.wait()
        self.part[...] = total(self.cross, self.count)
        self.own = pltpu.make_async_copy(self.part, self.final(self.me), self.local_sem)
        self.own.start()
        self.copies = []
        for s in range(1, PEERS):
            copy = remote(self.part, self.final(self.me), *self.back_sems, s, self.in_plane(s)[1])
            copy.start()
            self.copies.append(copy)

    def finish(self):
        self.own.wait()
        for copy in self.copies:
            copy.wait()


class CoreSum(PlaneSum):
    def __init__(self, axes, grads, got, halves, final, core_sems, terms, part, cross, *sems):
        self.grads, self.got, self.halves, self.whole, self.core_sems = grads, got, halves, final, core_sems
        core = place()[3]
        super().__init__(axes, lambda p: halves.at[p], terms, part, cross, lambda p: final.at[core * PEERS + p], *sems)
        self.core = core
        self.other = device_at(*self.at[:3], 1 - core)

    def partners(self):
        return [self.other] + super().partners()

    def start_core(self):
        self.swap = remote(self.grads.at[pl.ds((1 - self.core) * PEERS, PEERS)], self.got, *self.core_sems, 0, self.other)
        self.swap.start()

    def start(self):
        self.swap.wait()
        for p in range(PEERS):
            self.halves[p] = (self.grads[self.core * PEERS + p].astype(F32) + self.got[p].astype(F32)).astype(BF)
        super().start()

    def finish(self):
        super().finish()
        mine = self.whole.at[pl.ds(self.core * PEERS, PEERS)]
        self.swap = remote(mine, mine, *self.core_sems, 1, self.other)
        self.swap.start()

    def finish_core(self):
        self.swap.wait()


def put_tiles(ref, rows, first, value):
    done = 0
    while done < value.shape[0]:
        piece, row = divmod(first + done, rows)
        count = min(rows - row, value.shape[0] - done)
        ref[piece, row:row + count, :] = value[done:done + count]
        done += count


def get_tiles(ref, rows, first, count):
    parts, done = [], 0
    while done < count:
        piece, row = divmod(first + done, rows)
        take = min(rows - row, count - done)
        parts.append(ref[piece, row:row + take, :].astype(F32))
        done += take
    return parts[0] if len(parts) == 1 else jnp.concatenate(parts, axis=0)


def block_kernel(
    field_ref, cot_ref, *refs,
):
    count = 14
    sources, outs, (held, rest) = refs[:count], refs[count:count + 5], (refs[count + 5:2 * count + 5], refs[2 * count + 5:])
    block(field_ref, cot_ref, sources, held, *outs, *rest)


def block(
    field_ref, cot_ref, sources, held,
    mixed_out, fgrad_out, final0, final1, final_t,
    x_ref, t_ref, bias_ref, z_ref, p_ref, qblk_ref, q_ref, k_ref, v_ref, kv_ref, ctx_ref, dctx_ref, dproj_ref,
    win_ref, send_ref, grads0, grads1, grads_t, got0, got1, halves0, halves1,
    terms0, terms1, terms_t, part0, part1, part_t, cross0, cross1, cross_t,
    load_sems, local_sems, halo_send, halo_recv, trail_send, trail_recv, core_send, core_recv,
    plane_send, plane_recv, x_send, x_recv, back_send, back_recv,
):
    gain_attn, gain_mlp, qkv_w, proj_w, fc1_w, fc2_w, table, perm, expand, head_mask, rep, pair, entry, differs = held
    lon, lat = lax.axis_index("lon"), lax.axis_index("lat")
    lon_n, lat_n = 32, 4
    west, east = (lon + lon_n - 1) % lon_n, (lon + 1) % lon_n
    above, below = (lat + lat_n - 1) % lat_n, (lat + 1) % lat_n

    sum0, sum1 = [
        CoreSum(
            axes, grads, got, halves, final, (core_send.at[k], core_recv.at[k]), terms, part, cross,
            (plane_send.at[k], plane_recv.at[k]), (x_send.at[k], x_recv.at[k]), (back_send.at[k], back_recv.at[k]), local_sems.at[4 + k],
        )
        for k, (axes, grads, got, halves, final, terms, part, cross) in enumerate((
            ((0, 1, 2), grads0, got0, halves0, final0, terms0, part0, cross0),
            ((0, 2, 1), grads1, got1, halves1, final1, terms1, part1, cross1),
        ))
    ]
    sum_t = PlaneSum(
        (1, 2, 0), lambda p: grads_t.at[p], terms_t, part_t, cross_t, lambda p: final_t.at[p],
        (plane_send.at[2], plane_recv.at[2]), (x_send.at[2], x_recv.at[2]), (back_send.at[2], back_recv.at[2]), local_sems.at[6],
    )

    barrier = pltpu.get_barrier_semaphore()
    partners = [(west, lat), (east, lat), (lon, above), (lon, below), (west, above), (east, below)]
    partners += sum_t.partners() + sum0.partners() + sum1.partners()
    for device in partners:
        pl.semaphore_signal(barrier, inc=1, device_id=device, device_id_type=MESH_ID)
    loads = [pltpu.make_async_copy(a, b, load_sems.at[k]) for k, (a, b) in enumerate(zip(sources, held))]
    first = (6, 11, 10, 12, 13)
    for k in first + tuple(k for k in range(len(loads)) if k not in first):
        loads[k].start()
    pl.semaphore_wait(barrier, len(partners))

    right, left = pl.ds(HALF, HALF), pl.ds(0, HALF)
    upper, lower = pl.ds(0, 3), pl.ds(3, 3)
    halos = []
    for k, source in enumerate((field_ref, cot_ref)):
        win = win_ref.at[k]
        copies = [pltpu.make_async_copy(source.at[lower, :, right], win.at[upper, :, left], local_sems.at[k])]
        for s, (rows, cols, device) in enumerate((((lower, upper), (left, right), (west, lat)), ((upper, lower), (right, left), (lon, above)), ((upper, lower), (left, right), (west, above)))):
            copies.append(remote(source.at[rows[0], :, cols[0]], win.at[rows[1], :, cols[1]], halo_send, halo_recv, 3 * k + s, device))
        halos.append(copies)
    for copy in halos[0]:
        copy.start()

    def trail(value, k, out):
        win = send_ref.at[k]
        back = nt(perm[...], value)
        for c in range(WC):
            win[:, :, c * C:(c + 1) * C] = back[c * 48:(c + 1) * 48].reshape(WR, 8, C).astype(BF)
        copies = [pltpu.make_async_copy(win.at[upper, :, left], out.at[lower, :, right], local_sems.at[2 + k])]
        for s, (rows, cols, device) in enumerate((((upper, lower), (right, left), (east, lat)), ((lower, upper), (left, right), (lon, below)), ((lower, upper), (right, left), (east, below)))):
            copies.append(remote(win.at[rows[0], :, cols[0]], out.at[rows[1], :, cols[1]], trail_send, trail_recv, 3 * k + s, device))
        for copy in copies:
            copy.start()
        return copies

    for k in first:
        loads[k].wait()
    t_ref[...] = jnp.zeros_like(t_ref)
    for w in range(NW):
        for h in range(HEADS):
            t_ref[h * RELP:h * RELP + REL, :] = table[w, h, :, 0, :]
        rest = t_ref[...]
        spread = None
        for part in range(3):
            low = rest.astype(BF)
            rest = rest - low.astype(F32)
            moved = nn(low, pair[...]).astype(BF)
            term = tn(moved, rep[...])
            spread = term if spread is None else spread + term
        z = spread[0:16] * entry[0:1]
        for a in range(1, A):
            z = z + spread[16 * a:16 * a + 16] * entry[a:a + 1]
        hide = jnp.where(lat == lat_n - 1, differs[1], 0.0)
        if w == NW - 1:
            hide = hide + differs[0]
        z = jnp.where(hide > 0.5, MASKED, z)
        for cs in range(WC):
            bias_ref[w, cs * A:(cs + 1) * A, :] = z[0:A, (11 - cs) * HEADS * A:(11 - cs) * HEADS * A + HT]

    for k in range(len(loads)):
        if k not in first:
            loads[k].wait()
    for copy in halos[0]:
        copy.wait()
    for copy in halos[1]:
        copy.start()
    field = tn(tokens_of(x_ref, win_ref.at[0]), perm[...])

    gain1 = column_of(gain_attn[...])
    gain2 = column_of(gain_mlp[...])
    hat1, inv1 = normalise(field)
    normed1 = (hat1 * gain1).astype(BF)
    projected = tn(qkv_w[...], normed1)
    scaling = HEAD ** (-0.5)
    q_ref[...] = (projected[0:C] * scaling).astype(BF)
    k_ref[...] = projected[C:2 * C].astype(BF)
    v_ref[...] = projected[2 * C:].astype(BF)
    kv_ref[...] = tn(normed1, qkv_w[:, C:]).astype(BF)
    mask = head_mask[...].astype(F32)

    for w in range(NW):
        rows = slice(w * TW, (w + 1) * TW)
        qblk = (nn(q_ref[:, rows], expand[...]) * mask).astype(BF)
        qblk_ref[w] = qblk
        scores = nn(kv_ref[rows, 0:C], qblk) + bias_ref[w]
        raised = jnp.exp(scores - jnp.max(scores, axis=0, keepdims=True))
        probs = raised * (1.0 / jnp.sum(raised, axis=0, keepdims=True))
        p_ref[w] = probs
        context = (nn(v_ref[:, rows], probs.astype(BF)) * mask).astype(BF)
        ctx_ref[:, rows] = nt(context, expand[...]).astype(BF)
    attended = tn(proj_w[...], ctx_ref[...]).astype(BF)

    for copy in halos[1]:
        copy.wait()
    cot = tn(tokens_of(x_ref, win_ref.at[1]), perm[...])
    cot_low = cot.astype(BF)

    resid = field + attended.astype(F32)
    hat2, inv2 = normalise(resid)
    normed2 = (hat2 * gain2).astype(BF)
    hidden = tn(fc1_w[...], normed2)
    k0 = 0.7978845608028654
    k1 = 0.044715
    sq = hidden * hidden
    th = jnp.tanh(hidden * (k0 + (k0 * k1) * sq))
    half = 0.5 * (1.0 + th)
    act = (hidden * half).astype(BF)
    slope = half + 0.5 * hidden * (1.0 - th * th) * (k0 + (3.0 * k0 * k1) * sq)
    d_act = tn(fc2_w[...], cot_low).astype(BF)
    d_pre = (d_act.astype(F32) * slope).astype(BF)
    fc1_grad = nt(normed2, d_pre).astype(BF)
    fc2_grad = nt(cot_low, act).astype(BF)
    for k in range(6):
        put_tiles(grads0, ROWS[0], k * C, fc1_grad[:, k * LANES:(k + 1) * LANES])
        put_tiles(grads0, ROWS[0], (6 + k) * C, fc2_grad[:, k * LANES:(k + 1) * LANES])
    d_normed2 = nn(fc1_w[...], d_pre)
    gain2_grad = row_of(jnp.sum(d_normed2 * hat2, axis=1, keepdims=True))
    d_resid = cot + normalise_back(d_normed2 * gain2, hat2, inv2)
    d_att = d_resid.astype(BF)
    proj_grad = nt(ctx_ref[...], d_att).astype(BF)
    put_tiles(grads0, ROWS[0], 12 * C, proj_grad[:, C - LANES:])
    gain_rows = jnp.concatenate([gain2_grad[:, 0:LANES], gain2_grad[:, C - LANES:], jnp.zeros((62, LANES), F32)], axis=0)
    put_tiles(grads0, ROWS[0], 13 * C, gain_rows.astype(BF))
    sum0.start_core()
    dctx_ref[...] = nn(proj_w[...], d_att).astype(BF)

    for w in range(NW):
        if w == 2:
            sum0.start()
        rows = slice(w * TW, (w + 1) * TW)
        dblk = (nn(dctx_ref[:, rows], expand[...]) * mask).astype(BF)
        probs = p_ref[w]
        d_probs = nn(kv_ref[rows, C:], dblk)
        weighted = probs * d_probs
        d_scores = weighted - probs * jnp.sum(weighted, axis=0, keepdims=True)
        d_low = d_scores.astype(BF)
        dproj_ref[2 * C:, rows] = nt(dblk, probs.astype(BF)).astype(BF)
        dproj_ref[C:2 * C, rows] = nt(qblk_ref[w], d_low).astype(BF)
        d_q = (nn(k_ref[:, rows], d_low) * (mask * scaling)).astype(BF)
        dproj_ref[0:C, rows] = nt(d_q, expand[...]).astype(BF)
        p_ref[w] = d_scores

    dproj = dproj_ref[...]
    qkv_grad = nt(normed1, dproj).astype(BF)
    d_win = nn(qkv_w[...], dproj).astype(BF).astype(F32)
    gain1_grad = row_of(jnp.sum(d_win * hat1, axis=1, keepdims=True))
    for k in range(4):
        put_tiles(grads1, ROWS[1], k * C, qkv_grad[:, k * LANES:(k + 1) * LANES])
    put_tiles(grads1, ROWS[1], 4 * C, jnp.concatenate([qkv_grad[:, 4 * LANES:], proj_grad[:, 0:64]], axis=1))
    gain_rows = jnp.concatenate([gain1_grad[:, 0:LANES], gain1_grad[:, C - LANES:], jnp.zeros((62, LANES), F32)], axis=0)
    put_tiles(grads1, ROWS[1], 5 * C, gain_rows.astype(BF))
    sum1.start_core()

    for w in range(NW):
        z_ref[...] = jnp.zeros_like(z_ref)
        for cs in range(WC):
            at = slice((11 - cs) * HEADS * A, (11 - cs) * HEADS * A + HT)
            z_ref[0:A, at] += p_ref[w, cs * A:(cs + 1) * A, :]
        dz = z_ref[...]
        spread = jnp.concatenate([dz * entry[a:a + 1] for a in range(A)], axis=0).astype(BF)
        d_table = nt(nt(rep[...], spread).astype(BF), pair[...]).astype(BF)
        for k in range(3):
            grads_t[3 * w + k] = d_table[TROWS * k:TROWS * (k + 1), 0:LANES]
            grads_t[12 + k, :, 16 * w:16 * w + 16] = d_table[TROWS * k:TROWS * (k + 1), LANES:]
        if w == 1:
            sum1.start()
    for k in range(3):
        grads_t[12 + k, :, 64:] = jnp.zeros((TROWS, 64), BF)
    grads_t[15] = jnp.zeros((TROWS, LANES), BF)
    sum_t.start()

    d_field = (d_resid + normalise_back(d_win * gain1, hat1, inv1)).astype(BF)
    fgrad_copies = trail(d_field, 1, fgrad_out)
    sum0.across()
    mixed = (resid + nn(fc2_w[...], act)).astype(BF)
    mixed_copies = trail(mixed, 0, mixed_out)
    sum1.across()
    sum0.back()
    sum_t.across()
    sum1.back()
    sum_t.back()
    sum0.finish()
    sum1.finish()
    sum_t.finish()
    sum0.finish_core()
    sum1.finish_core()
    for copy in mixed_copies + fgrad_copies:
        copy.wait()


def results_kernel(
    mixed_in, fgrad_in, final0_in, final1_in, final_t_in,
    mixed, fgrad, qkv, proj, fc1, fc2, gain_attn, gain_mlp, table,
    final0, final1, final_t, through, sems,
):
    copies = [pltpu.make_async_copy(a, b, sems.at[k]) for k, (a, b) in enumerate((
        (mixed_in, through.at[0]), (fgrad_in, through.at[1]), (final0_in, final0), (final1_in, final1), (final_t_in, final_t),
    ))]
    for copy in copies:
        copy.start()
    outward = []
    for k, out in enumerate((mixed, fgrad)):
        copies[k].wait()
        outward.append(pltpu.make_async_copy(through.at[k], out, sems.at[5 + k]))
        outward[k].start()
    for copy in copies[2:]:
        copy.wait()
    for k in range(6):
        fc1[:, k * LANES:(k + 1) * LANES] = get_tiles(final0, ROWS[0], k * C, C)
        fc2[:, k * LANES:(k + 1) * LANES] = get_tiles(final0, ROWS[0], (6 + k) * C, C)
    proj[:, 64:] = get_tiles(final0, ROWS[0], 12 * C, C)
    for k in range(4):
        qkv[:, k * LANES:(k + 1) * LANES] = get_tiles(final1, ROWS[1], k * C, C)
    shared = get_tiles(final1, ROWS[1], 4 * C, C)
    qkv[:, 4 * LANES:] = shared[:, 0:64]
    proj[:, 0:64] = shared[:, 64:]
    for out, final, row in ((gain_attn, final1, 5 * C), (gain_mlp, final0, 13 * C)):
        rows = get_tiles(final, final.shape[1], row, 16)
        out[:, 0:LANES] = rows[0:1]
        out[:, LANES:] = rows[1:2, 64:]
    for w in range(NW):
        wide = jnp.concatenate([final_t[3 * w + k].astype(F32) for k in range(3)], axis=0)
        tail = jnp.concatenate([final_t[12 + k].astype(F32) for k in range(3)], axis=0)
        for h in range(HEADS):
            table[w, h, :, 0, 0:LANES] = wide[h * RELP:h * RELP + REL]
            table[w, h, :, 0, LANES:] = tail[h * RELP:h * RELP + REL, 16 * w:16 * w + 16]
    for copy in outward:
        copy.wait()


def shards(field, cotangent, gain_attn, gain_mlp, qkv_weight, proj_weight, fc1_weight, fc2_weight, bias_table):
    consts = [jnp.asarray(v) for v in constants()]
    sds = jax.ShapeDtypeStruct
    vm = pl.BlockSpec(memory_space=pltpu.VMEM)
    hbm = pl.BlockSpec(memory_space=pl.ANY)
    levels, rows, flat = field.shape
    tile = (rows, levels, flat)
    dma = pltpu.SemaphoreType.DMA
    operands = [
        field.transpose(1, 0, 2), cotangent.transpose(1, 0, 2), gain_attn.reshape(1, C), gain_mlp.reshape(1, C),
        qkv_weight, proj_weight, fc1_weight, fc2_weight.T, bias_table.transpose(0, 2, 3, 1, 4), *consts,
    ]
    pieces = pl.pallas_call(
        block_kernel,
        out_shape=(
            sds(tile, BF), sds(tile, BF),
            sds((2 * PEERS, ROWS[0], LANES), BF), sds((2 * PEERS, ROWS[1], LANES), BF), sds((PEERS, TROWS, LANES), BF),
        ),
        in_specs=[hbm] * len(operands),
        out_specs=(hbm,) * 5,
        scratch_shapes=[pltpu.VMEM(v.shape, v.dtype) for v in operands[2:]] + [
            pltpu.VMEM((TOK, C), F32),
            pltpu.VMEM((HEADS * RELP, TW), F32),
            pltpu.VMEM((NW, TW, HT), F32),
            pltpu.VMEM((16, ZL), F32),
            pltpu.VMEM((NW, TW, HT), F32),
            pltpu.VMEM((NW, C, HT), BF),
            pltpu.VMEM((C, TOK), BF), pltpu.VMEM((C, TOK), BF), pltpu.VMEM((C, TOK), BF),
            pltpu.VMEM((TOK, 2 * C), BF),
            pltpu.VMEM((C, TOK), BF), pltpu.VMEM((C, TOK), BF),
            pltpu.VMEM((3 * C, TOK), BF),
            pltpu.VMEM((2,) + tile, BF),
            pltpu.VMEM((2,) + tile, BF),
            pltpu.VMEM((2 * PEERS, ROWS[0], LANES), BF), pltpu.VMEM((2 * PEERS, ROWS[1], LANES), BF), pltpu.VMEM((PEERS, TROWS, LANES), BF),
            pltpu.VMEM((PEERS, ROWS[0], LANES), BF), pltpu.VMEM((PEERS, ROWS[1], LANES), BF),
            pltpu.VMEM((PEERS, ROWS[0], LANES), BF), pltpu.VMEM((PEERS, ROWS[1], LANES), BF),
            pltpu.VMEM((PEERS, ROWS[0], LANES), BF), pltpu.VMEM((PEERS, ROWS[1], LANES), BF), pltpu.VMEM((PEERS, TROWS, LANES), BF),
            pltpu.VMEM((ROWS[0], LANES), BF), pltpu.VMEM((ROWS[1], LANES), BF), pltpu.VMEM((TROWS, LANES), BF),
            pltpu.VMEM((4, ROWS[0], LANES), BF), pltpu.VMEM((4, ROWS[1], LANES), BF), pltpu.VMEM((2, TROWS, LANES), BF),
            dma((len(operands) - 2,)), dma((7,)), dma((6,)), dma((6,)), dma((6,)), dma((6,)), dma((2, 2)), dma((2, 2)),
            dma((3, PEERS)), dma((3, PEERS)), dma((3, 4)), dma((3, 4)), dma((3, PEERS)), dma((3, PEERS)),
        ],
        compiler_params=pltpu.CompilerParams(vmem_limit_bytes=56 * 1024 * 1024, collective_id=0, has_side_effects=True),
        name="block",
    )(
        *operands
    )
    mixed, fgrad, qkv, proj, fc1, fc2, gain1, gain2, table = pl.pallas_call(
        results_kernel,
        out_shape=(
            sds(tile, BF), sds(tile, BF), sds((C, 3 * C), F32), sds((C, C), F32), sds((C, HID), F32), sds((C, HID), F32),
            sds((1, C), F32), sds((1, C), F32), sds((NW, HEADS, REL, 1, TW), F32),
        ),
        in_specs=[hbm] * 5,
        out_specs=(hbm,) * 2 + (vm,) * 7,
        scratch_shapes=[
            pltpu.VMEM((2 * PEERS, ROWS[0], LANES), BF), pltpu.VMEM((2 * PEERS, ROWS[1], LANES), BF), pltpu.VMEM((PEERS, TROWS, LANES), BF),
            pltpu.VMEM((2,) + tile, BF),
            dma((7,)),
        ],
        compiler_params=pltpu.CompilerParams(vmem_limit_bytes=60 * 1024 * 1024),
        name="results",
    )(*pieces)
    return (
        mixed.transpose(1, 0, 2), fgrad.transpose(1, 0, 2), qkv, proj, fc1, fc2.T,
        gain1.reshape(C), gain2.reshape(C), table.transpose(0, 3, 1, 2, 4),
    )


def solution(mesh):
    grid = P(None, "lat", "lon")
    by_type = P(None, "lat", None, None, None)
    return jax.shard_map(
        shards,
        mesh=mesh,
        in_specs=(grid, grid) + (P(),) * 6 + (by_type,),
        out_specs=(grid, grid) + (P(),) * 6 + (by_type,),
        check_vma=False,
    )
```

time: 95.6 us -> 60.1 us (0.63)
  Pallas kernels: 79.5 us -> 58.6 us
  local copies, waits for them, and re-layouts: 15 us -> 0 us
    pallas_call x1, Pallas kernels: 78 us -> 54.9 us  [shards(): pl.pallas_call(block_kernel, out_shape=(sds(tile, BF), sds(tile, BF), sds...]
    unnamed x28 -> x0, local copies, waits for them, and re-layouts: 15 us -> none
    pallas_call x1, Pallas kernels: 1.53 us -> 3.67 us  [shards(): pl.pallas_call(results_kernel, out_shape=(sds(tile, BF), sds(tile, BF), s...]
where the time goes in v2:
time: 60.1 us; the launch traced here: 59.4 us
  Pallas kernels  58.6 us (98%)
  between operations  0.81 us (1%)
    pallas_call x1, Pallas kernels, shards(): pl.pallas_call(block_kernel, out_shape=(sds(tile, BF), sds(tile, BF), sds...  54.9 us
    pallas_call x1, Pallas kernels, shards(): pl.pallas_call(results_kernel, out_shape=(sds(tile, BF), sds(tile, BF), s...  3.67 us

profile of v2, /device:TPU:1, one launch (start us, length us, event | category | flops | bytes accessed | tf_op | source)
XLA Modules:
  0.0 59.4 jit_solution(7346495781301548588)
XLA Ops:
  0.6 54.9 %block.1 = (bf16[6,8,2304]{2,1,0:T(8,128)(2,1)}, bf16[6,8,2304]{2,1,0:T(8,128)(2,1)}, bf16[32,80,128]{2,1,0:T(8,128)(2,1)}, bf16[32,32,128]{2,1,0:T(8,128)(2,1)}, bf16[16,48,128]{2,1,0:T(8,128)(2,1)}) custom-call(bf16[6,8,2304]{2,1,0:T(8,128)(2,1)} %bitcast.14, bf16[6,8,2304]{2,1,0:T(8,128)(2,1)} %bitcast.15, f32[1,192]{1,0:T(1,128)} %bitcast.16, ...), custom_call_target="tpu_custom_call" | custom-call | tf_op jit(solution)/shard_map/block/pallas_call | solution.py:531
  55.6 3.7 %results.1 = (bf16[6,8,2304]{2,1,0:T(8,128)(2,1)}, bf16[6,8,2304]{2,1,0:T(8,128)(2,1)}, f32[192,576]{1,0:T(8,128)}, f32[192,192]{1,0:T(8,128)}, f32[192,768]{1,0...) custom-call(bf16[6,8,2304]{2,1,0:T(8,128)(2,1)} %get-tuple-element.23.mixed, ...), custom_call_target="tpu_custom_call" | custom-call | tf_op jit(solution)/shard_map/results/pallas_call | solution.py:566

commit v3 on v2

--- a/solution.py
+++ b/solution.py
@@ -122,10 +122,14 @@
     return ((y * 2 + x // 2) * 4 + z, x % 2 * 2 + core)
 
 
-def remote(src, dst, sends, recvs, k, device):
+def remote(src, dst, send_sem, recv_sem, device):
     return pltpu.make_async_remote_copy(
-        src_ref=src, dst_ref=dst, send_sem=sends.at[k], recv_sem=recvs.at[k], device_id=device, device_id_type=MESH_ID
+        src_ref=src, dst_ref=dst, send_sem=send_sem, recv_sem=recv_sem, device_id=device, device_id_type=MESH_ID
     )
+
+
+def drain(like, sem):
+    pltpu.make_async_copy(like, like, sem).wait()
 
 
 def total(ref, count):
@@ -136,14 +140,16 @@
 
 
 class PlaneSum:
-    def __init__(self, axes, piece, terms, part, cross, final, plane_sems, x_sems, back_sems, local_sem):
+    def __init__(self, axes, piece, terms, part, cross, final, sends, recvs):
         self.axes, self.piece, self.terms, self.part, self.cross, self.final = axes, piece, terms, part, cross, final
-        self.plane_sems, self.x_sems, self.back_sems, self.local_sem = plane_sems, x_sems, back_sems, local_sem
+        self.sends, self.recvs = sends, recvs
         self.at = place()
         self.me = self.at[axes[0]] * 4 + self.at[axes[1]]
         self.count = cross.shape[0]
         self.step = 4 // self.count
         self.mine = self.at[axes[2]] // self.step
+        self.others = terms.at[pl.ds(1, PEERS - 1)]
+        self.few = cross.at[pl.ds(1, self.count - 1)]
 
     def in_plane(self, s):
         p = (self.me + s) % PEERS
@@ -156,61 +162,49 @@
         at[self.axes[2]] = (at[self.axes[2]] + s * self.step) % 4
         return device_at(*at)
 
-    def partners(self):
-        return [self.in_plane(s)[1] for s in range(1, PEERS)] + [self.along(s) for s in range(1, self.count)]
-
     def start(self):
-        self.copies = []
         for s in range(1, PEERS):
             p, device = self.in_plane(s)
-            copy = remote(self.piece(p), self.terms.at[s], *self.plane_sems, s, device)
-            copy.start()
-            self.copies.append(copy)
+            remote(self.piece(p), self.terms.at[s], self.sends.at[0], self.recvs.at[0], device).start()
 
     def across(self):
         self.terms[0] = self.piece(self.me)[...]
-        for copy in self.copies:
-            copy.wait()
+        drain(self.others, self.recvs.at[0])
         value = total(self.terms, PEERS)
-        self.part[...] = value
+        self.part[0] = value
         self.cross[self.mine] = value
-        self.copies = []
         for s in range(1, self.count):
-            copy = remote(self.part, self.cross.at[self.mine], *self.x_sems, s, self.along(s))
-            copy.start()
-            self.copies.append(copy)
+            remote(self.part.at[0], self.cross.at[self.mine], self.sends.at[1], self.recvs.at[1], self.along(s)).start()
 
     def back(self):
-        for copy in self.copies:
-            copy.wait()
-        self.part[...] = total(self.cross, self.count)
-        self.own = pltpu.make_async_copy(self.part, self.final(self.me), self.local_sem)
-        self.own.start()
-        self.copies = []
+        drain(self.few, self.recvs.at[1])
+        value = total(self.cross, self.count)
+        self.part[1] = value
+        self.final[self.first + self.me] = value
         for s in range(1, PEERS):
-            copy = remote(self.part, self.final(self.me), *self.back_sems, s, self.in_plane(s)[1])
-            copy.start()
-            self.copies.append(copy)
+            remote(self.part.at[1], self.final.at[self.first + self.me], self.sends.at[2], self.recvs.at[2], self.in_plane(s)[1]).start()
 
     def finish(self):
-        self.own.wait()
-        for copy in self.copies:
-            copy.wait()
+        drain(self.others, self.recvs.at[2])
+
+    def finish_sends(self):
+        drain(self.others, self.sends.at[0])
+        drain(self.few, self.sends.at[1])
+        drain(self.others, self.sends.at[2])
+
+    first = 0
 
 
 class CoreSum(PlaneSum):
-    def __init__(self, axes, grads, got, halves, final, core_sems, terms, part, cross, *sems):
-        self.grads, self.got, self.halves, self.whole, self.core_sems = grads, got, halves, final, core_sems
-        core = place()[3]
-        super().__init__(axes, lambda p: halves.at[p], terms, part, cross, lambda p: final.at[core * PEERS + p], *sems)
-        self.core = core
-        self.other = device_at(*self.at[:3], 1 - core)
-
-    def partners(self):
-        return [self.other] + super().partners()
+    def __init__(self, axes, grads, got, halves, final, core_sems, *args):
+        self.grads, self.got, self.halves, self.core_sems = grads, got, halves, core_sems
+        super().__init__(axes, lambda p: halves.at[p], *args[:3], final, *args[3:])
+        self.core = self.at[3]
+        self.first = self.core * PEERS
+        self.other = device_at(*self.at[:3], 1 - self.core)
 
     def start_core(self):
-        self.swap = remote(self.grads.at[pl.ds((1 - self.core) * PEERS, PEERS)], self.got, *self.core_sems, 0, self.other)
+        self.swap = remote(self.grads.at[pl.ds((1 - self.core) * PEERS, PEERS)], self.got, self.core_sems[0].at[0], self.core_sems[1].at[0], self.other)
         self.swap.start()
 
     def start(self):
@@ -221,8 +215,8 @@
 
     def finish(self):
         super().finish()
-        mine = self.whole.at[pl.ds(self.core * PEERS, PEERS)]
-        self.swap = remote(mine, mine, *self.core_sems, 1, self.other)
+        mine = self.final.at[pl.ds(self.first, PEERS)]
+        self.swap = remote(mine, mine, self.core_sems[0].at[1], self.core_sems[1].at[1], self.other)
         self.swap.start()
 
     def finish_core(self):
@@ -263,7 +257,7 @@
     win_ref, send_ref, grads0, grads1, grads_t, got0, got1, halves0, halves1,
     terms0, terms1, terms_t, part0, part1, part_t, cross0, cross1, cross_t,
     load_sems, local_sems, halo_send, halo_recv, trail_send, trail_recv, core_send, core_recv,
-    plane_send, plane_recv, x_send, x_recv, back_send, back_recv,
+    sum_send, sum_recv,
 ):
     gain_attn, gain_mlp, qkv_w, proj_w, fc1_w, fc2_w, table, perm, expand, head_mask, rep, pair, entry, differs = held
     lon, lat = lax.axis_index("lon"), lax.axis_index("lat")
@@ -272,23 +266,16 @@
     above, below = (lat + lat_n - 1) % lat_n, (lat + 1) % lat_n
 
     sum0, sum1 = [
-        CoreSum(
-            axes, grads, got, halves, final, (core_send.at[k], core_recv.at[k]), terms, part, cross,
-            (plane_send.at[k], plane_recv.at[k]), (x_send.at[k], x_recv.at[k]), (back_send.at[k], back_recv.at[k]), local_sems.at[4 + k],
-        )
-        for k, (axes, grads, got, halves, final, terms, part, cross) in enumerate((
-            ((0, 1, 2), grads0, got0, halves0, final0, terms0, part0, cross0),
-            ((0, 2, 1), grads1, got1, halves1, final1, terms1, part1, cross1),
+        CoreSum((0, 1, 2), grads, got, halves, final, (core_send.at[k], core_recv.at[k]), terms, part, cross, sum_send.at[k], sum_recv.at[k])
+        for k, (grads, got, halves, final, terms, part, cross) in enumerate((
+            (grads0, got0, halves0, final0, terms0, part0, cross0), (grads1, got1, halves1, final1, terms1, part1, cross1),
         ))
     ]
-    sum_t = PlaneSum(
-        (1, 2, 0), lambda p: grads_t.at[p], terms_t, part_t, cross_t, lambda p: final_t.at[p],
-        (plane_send.at[2], plane_recv.at[2]), (x_send.at[2], x_recv.at[2]), (back_send.at[2], back_recv.at[2]), local_sems.at[6],
-    )
+    sum_t = PlaneSum((1, 2, 0), lambda p: grads_t.at[p], terms_t, part_t, cross_t, final_t, sum_send.at[2], sum_recv.at[2])
 
     barrier = pltpu.get_barrier_semaphore()
     partners = [(west, lat), (east, lat), (lon, above), (lon, below), (west, above), (east, below)]
-    partners += sum_t.partners() + sum0.partners() + sum1.partners()
+    partners += [sum0.other] + [sum0.in_plane(s)[1] for s in range(1, PEERS)] + [sum_t.in_plane(s)[1] for s in range(1, PEERS) if s % 4]
     for device in partners:
         pl.semaphore_signal(barrier, inc=1, device_id=device, device_id_type=MESH_ID)
     loads = [pltpu.make_async_copy(a, b, load_sems.at[k]) for k, (a, b) in enumerate(zip(sources, held))]
@@ -304,7 +291,7 @@
         win = win_ref.at[k]
         copies = [pltpu.make_async_copy(source.at[lower, :, right], win.at[upper, :, left], local_sems.at[k])]
         for s, (rows, cols, device) in enumerate((((lower, upper), (left, right), (west, lat)), ((upper, lower), (right, left), (lon, above)), ((upper, lower), (left, right), (west, above)))):
-            copies.append(remote(source.at[rows[0], :, cols[0]], win.at[rows[1], :, cols[1]], halo_send, halo_recv, 3 * k + s, device))
+            copies.append(remote(source.at[rows[0], :, cols[0]], win.at[rows[1], :, cols[1]], halo_send.at[3 * k + s], halo_recv.at[3 * k + s], device))
         halos.append(copies)
     for copy in halos[0]:
         copy.start()
@@ -316,7 +303,7 @@
             win[:, :, c * C:(c + 1) * C] = back[c * 48:(c + 1) * 48].reshape(WR, 8, C).astype(BF)
         copies = [pltpu.make_async_copy(win.at[upper, :, left], out.at[lower, :, right], local_sems.at[2 + k])]
         for s, (rows, cols, device) in enumerate((((upper, lower), (right, left), (east, lat)), ((lower, upper), (left, right), (lon, below)), ((lower, upper), (right, left), (east, below)))):
-            copies.append(remote(win.at[rows[0], :, cols[0]], out.at[rows[1], :, cols[1]], trail_send, trail_recv, 3 * k + s, device))
+            copies.append(remote(win.at[rows[0], :, cols[0]], out.at[rows[1], :, cols[1]], trail_send.at[3 * k + s], trail_recv.at[3 * k + s], device))
         for copy in copies:
             copy.start()
         return copies
@@ -410,6 +397,8 @@
     gain_rows = jnp.concatenate([gain2_grad[:, 0:LANES], gain2_grad[:, C - LANES:], jnp.zeros((62, LANES), F32)], axis=0)
     put_tiles(grads0, ROWS[0], 13 * C, gain_rows.astype(BF))
     sum0.start_core()
+    mixed = (resid + nn(fc2_w[...], act)).astype(BF)
+    mixed_copies = trail(mixed, 0, mixed_out)
     dctx_ref[...] = nn(proj_w[...], d_att).astype(BF)
 
     for w in range(NW):
@@ -460,8 +449,6 @@
     d_field = (d_resid + normalise_back(d_win * gain1, hat1, inv1)).astype(BF)
     fgrad_copies = trail(d_field, 1, fgrad_out)
     sum0.across()
-    mixed = (resid + nn(fc2_w[...], act)).astype(BF)
-    mixed_copies = trail(mixed, 0, mixed_out)
     sum1.across()
     sum0.back()
     sum_t.across()
@@ -472,27 +459,19 @@
     sum_t.finish()
     sum0.finish_core()
     sum1.finish_core()
+    for each in (sum0, sum1, sum_t):
+        each.finish_sends()
     for copy in mixed_copies + fgrad_copies:
         copy.wait()
 
 
 def results_kernel(
-    mixed_in, fgrad_in, final0_in, final1_in, final_t_in,
-    mixed, fgrad, qkv, proj, fc1, fc2, gain_attn, gain_mlp, table,
-    final0, final1, final_t, through, sems,
+    mixed_in, fgrad_in, final0, final1, final_t,
+    mixed, fgrad, qkv, proj, fc1, fc2, gain_attn, gain_mlp, table, sems,
 ):
-    copies = [pltpu.make_async_copy(a, b, sems.at[k]) for k, (a, b) in enumerate((
-        (mixed_in, through.at[0]), (fgrad_in, through.at[1]), (final0_in, final0), (final1_in, final1), (final_t_in, final_t),
-    ))]
-    for copy in copies:
+    outward = [pltpu.make_async_copy(a, b, sems.at[k]) for k, (a, b) in enumerate(((mixed_in, mixed), (fgrad_in, fgrad)))]
+    for copy in outward:
         copy.start()
-    outward = []
-    for k, out in enumerate((mixed, fgrad)):
-        copies[k].wait()
-        outward.append(pltpu.make_async_copy(through.at[k], out, sems.at[5 + k]))
-        outward[k].start()
-    for copy in copies[2:]:
-        copy.wait()
     for k in range(6):
         fc1[:, k * LANES:(k + 1) * LANES] = get_tiles(final0, ROWS[0], k * C, C)
         fc2[:, k * LANES:(k + 1) * LANES] = get_tiles(final0, ROWS[0], (6 + k) * C, C)
@@ -535,7 +514,7 @@
             sds((2 * PEERS, ROWS[0], LANES), BF), sds((2 * PEERS, ROWS[1], LANES), BF), sds((PEERS, TROWS, LANES), BF),
         ),
         in_specs=[hbm] * len(operands),
-        out_specs=(hbm,) * 5,
+        out_specs=(vm,) * 5,
         scratch_shapes=[pltpu.VMEM(v.shape, v.dtype) for v in operands[2:]] + [
             pltpu.VMEM((TOK, C), F32),
             pltpu.VMEM((HEADS * RELP, TW), F32),
@@ -553,15 +532,15 @@
             pltpu.VMEM((PEERS, ROWS[0], LANES), BF), pltpu.VMEM((PEERS, ROWS[1], LANES), BF),
             pltpu.VMEM((PEERS, ROWS[0], LANES), BF), pltpu.VMEM((PEERS, ROWS[1], LANES), BF),
             pltpu.VMEM((PEERS, ROWS[0], LANES), BF), pltpu.VMEM((PEERS, ROWS[1], LANES), BF), pltpu.VMEM((PEERS, TROWS, LANES), BF),
-            pltpu.VMEM((ROWS[0], LANES), BF), pltpu.VMEM((ROWS[1], LANES), BF), pltpu.VMEM((TROWS, LANES), BF),
+            pltpu.VMEM((2, ROWS[0], LANES), BF), pltpu.VMEM((2, ROWS[1], LANES), BF), pltpu.VMEM((2, TROWS, LANES), BF),
             pltpu.VMEM((4, ROWS[0], LANES), BF), pltpu.VMEM((4, ROWS[1], LANES), BF), pltpu.VMEM((2, TROWS, LANES), BF),
             dma((len(operands) - 2,)), dma((7,)), dma((6,)), dma((6,)), dma((6,)), dma((6,)), dma((2, 2)), dma((2, 2)),
-            dma((3, PEERS)), dma((3, PEERS)), dma((3, 4)), dma((3, 4)), dma((3, PEERS)), dma((3, PEERS)),
+            dma((3, 3)), dma((3, 3)),
         ],
-        compiler_params=pltpu.CompilerParams(vmem_limit_bytes=56 * 1024 * 1024, collective_id=0, has_side_effects=True),
+        compiler_params=pltpu.CompilerParams(vmem_limit_bytes=36 * 1024 * 1024, collective_id=0, has_side_effects=True),
         name="block",
     )(
-        *operands
+        *[pltpu.with_memory_space_constraint(v, pltpu.HBM) for v in operands]
     )
     mixed, fgrad, qkv, proj, fc1, fc2, gain1, gain2, table = pl.pallas_call(
         results_kernel,
@@ -569,14 +548,10 @@
             sds(tile, BF), sds(tile, BF), sds((C, 3 * C), F32), sds((C, C), F32), sds((C, HID), F32), sds((C, HID), F32),
             sds((1, C), F32), sds((1, C), F32), sds((NW, HEADS, REL, 1, TW), F32),
         ),
-        in_specs=[hbm] * 5,
+        in_specs=[vm] * 5,
         out_specs=(hbm,) * 2 + (vm,) * 7,
-        scratch_shapes=[
-            pltpu.VMEM((2 * PEERS, ROWS[0], LANES), BF), pltpu.VMEM((2 * PEERS, ROWS[1], LANES), BF), pltpu.VMEM((PEERS, TROWS, LANES), BF),
-            pltpu.VMEM((2,) + tile, BF),
-            dma((7,)),
-        ],
-        compiler_params=pltpu.CompilerParams(vmem_limit_bytes=60 * 1024 * 1024),
+        scratch_shapes=[dma((2,))],
+        compiler_params=pltpu.CompilerParams(vmem_limit_bytes=16 * 1024 * 1024),
         name="results",
     )(*pieces)
     return (

time: 60.1 us -> 54.7 us (0.910)
  Pallas kernels: 58.6 us -> 53.8 us
    pallas_call x1, Pallas kernels: 54.9 us -> 51.5 us  [shards(): pl.pallas_call(block_kernel, out_shape=(sds(tile, BF), sds(tile, BF), sds...]
    pallas_call x1, Pallas kernels: 3.67 us -> 2.22 us  [shards(): pl.pallas_call(results_kernel, out_shape=(sds(tile, BF), sds(tile, BF), s...]
where the time goes in v3:
time: 54.7 us; the launch traced here: 54.6 us
  Pallas kernels  53.8 us (98%)
  between operations  0.81 us (1%)
    pallas_call x1, Pallas kernels, shards(): pl.pallas_call(block_kernel, out_shape=(sds(tile, BF), sds(tile, BF), sds...  51.5 us
    pallas_call x1, Pallas kernels, shards(): pl.pallas_call(results_kernel, out_shape=(sds(tile, BF), sds(tile, BF), s...  2.22 us

profile of v3, /device:TPU:1, one launch (start us, length us, event | category | flops | bytes accessed | tf_op | source)
XLA Modules:
  0.0 54.6 jit_solution(8477075128596184725)
XLA Ops:
  0.6 51.5 %block.1 = (bf16[6,8,2304]{2,1,0:T(8,128)(2,1)S(1)}, bf16[6,8,2304]{2,1,0:T(8,128)(2,1)S(1)}, bf16[32,80,128]{2,1,0:T(8,128)(2,1)S(1)}, bf16[32,32,128]{2,1,0:T(8,128)(2,1)S(1)}, bf16[16,48,128]{2,1,0:T(8,128)(2,1)S(1)}) custom-call(bf16[6,8,2304]{2,1,0:T(8,128)(2,1)} %bitcast.14, bf16[6,8,2304]{2,1,0:T(8,128)(2,1)} %bitcast.15, f32[1,192]{1,0:T(1,128)} %bitcast.16, ...), custom_call_target="tpu_custom_call" | custom-call | tf_op jit(solution)/shard_map/block/pallas_call | solution.py:510
  52.2 2.2 %results.1 = (bf16[6,8,2304]{2,1,0:T(8,128)(2,1)}, bf16[6,8,2304]{2,1,0:T(8,128)(2,1)}, f32[192,576]{1,0:T(8,128)}, f32[192,192]{1,0:T(8,128)}, f32[192,768]{1,0...) custom-call(bf16[6,8,2304]{2,1,0:T(8,128)(2,1)S(1)} %get-tuple-element.23.m, ...), custom_call_target="tpu_custom_call" | custom-call | tf_op jit(solution)/shard_map/results/pallas_call | solution.py:545

commit v4 on v3

--- a/solution.py
+++ b/solution.py
@@ -47,7 +47,7 @@
     for h in range(HEADS):
         for rel in range(REL):
             rep[h, rel, rel, h, :] = 1
-    rep = rep.reshape(HEADS * RELP, ZL)
+    rep = np.concatenate([rep.reshape(HEADS * RELP, ZL)] * 3)
     pair = np.zeros((WZ, WZ, WR, WR, WZ, WR, 16), np.float32)
     for lt in range(WZ):
         for ls in range(WZ):
@@ -257,7 +257,7 @@
     win_ref, send_ref, grads0, grads1, grads_t, got0, got1, halves0, halves1,
     terms0, terms1, terms_t, part0, part1, part_t, cross0, cross1, cross_t,
     load_sems, local_sems, halo_send, halo_recv, trail_send, trail_recv, core_send, core_recv,
-    sum_send, sum_recv,
+    sum_send, sum_recv, ready,
 ):
     gain_attn, gain_mlp, qkv_w, proj_w, fc1_w, fc2_w, table, perm, expand, head_mask, rep, pair, entry, differs = held
     lon, lat = lax.axis_index("lon"), lax.axis_index("lat")
@@ -275,12 +275,19 @@
 
     barrier = pltpu.get_barrier_semaphore()
     partners = [(west, lat), (east, lat), (lon, above), (lon, below), (west, above), (east, below)]
-    partners += [sum0.other] + [sum0.in_plane(s)[1] for s in range(1, PEERS)] + [sum_t.in_plane(s)[1] for s in range(1, PEERS) if s % 4]
+    chip = list(place())
+    lines = []
+    for axis in range(3):
+        for s in range(1, 4):
+            at = list(chip)
+            at[axis] = (at[axis] + s) % 4
+            lines.append(device_at(*at))
+    partners += [sum0.other] + lines
     for device in partners:
         pl.semaphore_signal(barrier, inc=1, device_id=device, device_id_type=MESH_ID)
     loads = [pltpu.make_async_copy(a, b, load_sems.at[k]) for k, (a, b) in enumerate(zip(sources, held))]
     first = (6, 11, 10, 12, 13)
-    for k in first + tuple(k for k in range(len(loads)) if k not in first):
+    for k in first:
         loads[k].start()
     pl.semaphore_wait(barrier, len(partners))
 
@@ -295,6 +302,9 @@
         halos.append(copies)
     for copy in halos[0]:
         copy.start()
+    for k in range(len(loads)):
+        if k not in first:
+            loads[k].start()
 
     def trail(value, k, out):
         win = send_ref.at[k]
@@ -310,18 +320,20 @@
 
     for k in first:
         loads[k].wait()
+    for device in lines:
+        pl.semaphore_signal(ready, inc=1, device_id=device, device_id_type=MESH_ID)
+
     t_ref[...] = jnp.zeros_like(t_ref)
     for w in range(NW):
         for h in range(HEADS):
             t_ref[h * RELP:h * RELP + REL, :] = table[w, h, :, 0, :]
         rest = t_ref[...]
-        spread = None
+        moved = []
         for part in range(3):
             low = rest.astype(BF)
             rest = rest - low.astype(F32)
-            moved = nn(low, pair[...]).astype(BF)
-            term = tn(moved, rep[...])
-            spread = term if spread is None else spread + term
+            moved.append(nn(low, pair[...]).astype(BF))
+        spread = tn(jnp.concatenate(moved, axis=0), rep[...])
         z = spread[0:16] * entry[0:1]
         for a in range(1, A):
             z = z + spread[16 * a:16 * a + 16] * entry[a:a + 1]
@@ -351,17 +363,17 @@
     k_ref[...] = projected[C:2 * C].astype(BF)
     v_ref[...] = projected[2 * C:].astype(BF)
     kv_ref[...] = tn(normed1, qkv_w[:, C:]).astype(BF)
-    mask = head_mask[...].astype(F32)
+    mask = head_mask[...]
 
     for w in range(NW):
         rows = slice(w * TW, (w + 1) * TW)
-        qblk = (nn(q_ref[:, rows], expand[...]) * mask).astype(BF)
+        qblk = nn(q_ref[:, rows], expand[...]).astype(BF) * mask
         qblk_ref[w] = qblk
         scores = nn(kv_ref[rows, 0:C], qblk) + bias_ref[w]
         raised = jnp.exp(scores - jnp.max(scores, axis=0, keepdims=True))
         probs = raised * (1.0 / jnp.sum(raised, axis=0, keepdims=True))
         p_ref[w] = probs
-        context = (nn(v_ref[:, rows], probs.astype(BF)) * mask).astype(BF)
+        context = nn(v_ref[:, rows], probs.astype(BF)).astype(BF) * mask
         ctx_ref[:, rows] = nt(context, expand[...]).astype(BF)
     attended = tn(proj_w[...], ctx_ref[...]).astype(BF)
 
@@ -402,10 +414,11 @@
     dctx_ref[...] = nn(proj_w[...], d_att).astype(BF)
 
     for w in range(NW):
-        if w == 2:
+        if w == 1:
+            pl.semaphore_wait(ready, len(lines))
             sum0.start()
         rows = slice(w * TW, (w + 1) * TW)
-        dblk = (nn(dctx_ref[:, rows], expand[...]) * mask).astype(BF)
+        dblk = nn(dctx_ref[:, rows], expand[...]).astype(BF) * mask
         probs = p_ref[w]
         d_probs = nn(kv_ref[rows, C:], dblk)
         weighted = probs * d_probs
@@ -413,7 +426,7 @@
         d_low = d_scores.astype(BF)
         dproj_ref[2 * C:, rows] = nt(dblk, probs.astype(BF)).astype(BF)
         dproj_ref[C:2 * C, rows] = nt(qblk_ref[w], d_low).astype(BF)
-        d_q = (nn(k_ref[:, rows], d_low) * (mask * scaling)).astype(BF)
+        d_q = (nn(k_ref[:, rows], d_low) * scaling).astype(BF) * mask
         dproj_ref[0:C, rows] = nt(d_q, expand[...]).astype(BF)
         p_ref[w] = d_scores
 
@@ -435,7 +448,7 @@
             z_ref[0:A, at] += p_ref[w, cs * A:(cs + 1) * A, :]
         dz = z_ref[...]
         spread = jnp.concatenate([dz * entry[a:a + 1] for a in range(A)], axis=0).astype(BF)
-        d_table = nt(nt(rep[...], spread).astype(BF), pair[...]).astype(BF)
+        d_table = nt(nt(rep[0:HEADS * RELP, :], spread).astype(BF), pair[...]).astype(BF)
         for k in range(3):
             grads_t[3 * w + k] = d_table[TROWS * k:TROWS * (k + 1), 0:LANES]
             grads_t[12 + k, :, 16 * w:16 * w + 16] = d_table[TROWS * k:TROWS * (k + 1), LANES:]
@@ -450,15 +463,15 @@
     fgrad_copies = trail(d_field, 1, fgrad_out)
     sum0.across()
     sum1.across()
-    sum0.back()
     sum_t.across()
     sum1.back()
+    sum0.back()
     sum_t.back()
+    sum1.finish()
     sum0.finish()
-    sum1.finish()
     sum_t.finish()
+    sum1.finish_core()
     sum0.finish_core()
-    sum1.finish_core()
     for each in (sum0, sum1, sum_t):
         each.finish_sends()
     for copy in mixed_copies + fgrad_copies:
@@ -467,30 +480,43 @@
 
 def results_kernel(
     mixed_in, fgrad_in, final0, final1, final_t,
-    mixed, fgrad, qkv, proj, fc1, fc2, gain_attn, gain_mlp, table, sems,
+    mixed_out, fgrad_out, qkv_out, proj_out, fc1_out, fc2_out, gain_attn_out, gain_mlp_out, table_out,
+    qkv, proj, fc1, fc2, gain_attn, gain_mlp, table, sems,
 ):
-    outward = [pltpu.make_async_copy(a, b, sems.at[k]) for k, (a, b) in enumerate(((mixed_in, mixed), (fgrad_in, fgrad)))]
-    for copy in outward:
-        copy.start()
+    outward = []
+
+    def send(value, out):
+        outward.append(pltpu.make_async_copy(value, out, sems.at[len(outward)]))
+        outward[-1].start()
+
+    send(mixed_in, mixed_out)
+    send(fgrad_in, fgrad_out)
+    for w in range(NW):
+        wide = jnp.concatenate([final_t[3 * w + k].astype(F32) for k in range(3)], axis=0)
+        tail = jnp.concatenate([final_t[12 + k].astype(F32) for k in range(3)], axis=0)
+        for h in range(HEADS):
+            table[w, h, :, 0, 0:LANES] = wide[h * RELP:h * RELP + REL]
+            table[w, h, :, 0, LANES:] = tail[h * RELP:h * RELP + REL, 16 * w:16 * w + 16]
+    send(table, table_out)
     for k in range(6):
         fc1[:, k * LANES:(k + 1) * LANES] = get_tiles(final0, ROWS[0], k * C, C)
+    send(fc1, fc1_out)
+    for k in range(6):
         fc2[:, k * LANES:(k + 1) * LANES] = get_tiles(final0, ROWS[0], (6 + k) * C, C)
+    send(fc2, fc2_out)
     proj[:, 64:] = get_tiles(final0, ROWS[0], 12 * C, C)
     for k in range(4):
         qkv[:, k * LANES:(k + 1) * LANES] = get_tiles(final1, ROWS[1], k * C, C)
     shared = get_tiles(final1, ROWS[1], 4 * C, C)
     qkv[:, 4 * LANES:] = shared[:, 0:64]
     proj[:, 0:64] = shared[:, 64:]
-    for out, final, row in ((gain_attn, final1, 5 * C), (gain_mlp, final0, 13 * C)):
+    send(qkv, qkv_out)
+    send(proj, proj_out)
+    for gain, out, final, row in ((gain_attn, gain_attn_out, final1, 5 * C), (gain_mlp, gain_mlp_out, final0, 13 * C)):
         rows = get_tiles(final, final.shape[1], row, 16)
-        out[:, 0:LANES] = rows[0:1]
-        out[:, LANES:] = rows[1:2, 64:]
-    for w in range(NW):
-        wide = jnp.concatenate([final_t[3 * w + k].astype(F32) for k in range(3)], axis=0)
-        tail = jnp.concatenate([final_t[12 + k].astype(F32) for k in range(3)], axis=0)
-        for h in range(HEADS):
-            table[w, h, :, 0, 0:LANES] = wide[h * RELP:h * RELP + REL]
-            table[w, h, :, 0, LANES:] = tail[h * RELP:h * RELP + REL, 16 * w:16 * w + 16]
+        gain[:, 0:LANES] = rows[0:1]
+        gain[:, LANES:] = rows[1:2, 64:]
+        send(gain, out)
     for copy in outward:
         copy.wait()
 
@@ -535,22 +561,20 @@
             pltpu.VMEM((2, ROWS[0], LANES), BF), pltpu.VMEM((2, ROWS[1], LANES), BF), pltpu.VMEM((2, TROWS, LANES), BF),
             pltpu.VMEM((4, ROWS[0], LANES), BF), pltpu.VMEM((4, ROWS[1], LANES), BF), pltpu.VMEM((2, TROWS, LANES), BF),
             dma((len(operands) - 2,)), dma((7,)), dma((6,)), dma((6,)), dma((6,)), dma((6,)), dma((2, 2)), dma((2, 2)),
-            dma((3, 3)), dma((3, 3)),
+            dma((3, 3)), dma((3, 3)), pltpu.SemaphoreType.REGULAR,
         ],
         compiler_params=pltpu.CompilerParams(vmem_limit_bytes=36 * 1024 * 1024, collective_id=0, has_side_effects=True),
         name="block",
     )(
         *[pltpu.with_memory_space_constraint(v, pltpu.HBM) for v in operands]
     )
+    shapes = [(C, 3 * C), (C, C), (C, HID), (C, HID), (1, C), (1, C), (NW, HEADS, REL, 1, TW)]
     mixed, fgrad, qkv, proj, fc1, fc2, gain1, gain2, table = pl.pallas_call(
         results_kernel,
-        out_shape=(
-            sds(tile, BF), sds(tile, BF), sds((C, 3 * C), F32), sds((C, C), F32), sds((C, HID), F32), sds((C, HID), F32),
-            sds((1, C), F32), sds((1, C), F32), sds((NW, HEADS, REL, 1, TW), F32),
-        ),
+        out_shape=[sds(tile, BF)] * 2 + [sds(v, F32) for v in shapes],
         in_specs=[vm] * 5,
-        out_specs=(hbm,) * 2 + (vm,) * 7,
-        scratch_shapes=[dma((2,))],
+        out_specs=[hbm] * 9,
+        scratch_shapes=[pltpu.VMEM(v, F32) for v in shapes] + [dma((9,))],
         compiler_params=pltpu.CompilerParams(vmem_limit_bytes=16 * 1024 * 1024),
         name="results",
     )(*pieces)

time: 54.7 us -> 54 us (0.987)
  Pallas kernels: 53.8 us -> 53.1 us
    pallas_call x1, Pallas kernels: 51.5 us -> 51 us  [shards(): pl.pallas_call(block_kernel, out_shape=(sds(tile, BF), sds(tile, BF), sds...]
where the time goes in v4:
time: 54 us; the launch traced here: 53.9 us
  Pallas kernels  53.1 us (98%)
  between operations  0.81 us (2%)
    pallas_call x1, Pallas kernels, shards(): pl.pallas_call(block_kernel, out_shape=(sds(tile, BF), sds(tile, BF), sds...  51 us
    pallas_call x1, Pallas kernels, shards(): pl.pallas_call(results_kernel, out_shape=[sds(tile, BF)] * 2 + [sds(v, F3...  2.13 us

profile of v4, /device:TPU:1, one launch (start us, length us, event | category | flops | bytes accessed | tf_op | source)
XLA Modules:
  0.0 53.9 jit_solution(2431093360834310101)
XLA Ops:
  0.6 51.0 %block.1 = (bf16[6,8,2304]{2,1,0:T(8,128)(2,1)S(1)}, bf16[6,8,2304]{2,1,0:T(8,128)(2,1)S(1)}, bf16[32,80,128]{2,1,0:T(8,128)(2,1)S(1)}, bf16[32,32,128]{2,1,0:T(8,128)(2,1)S(1)}, bf16[16,48,128]{2,1,0:T(8,128)(2,1)S(1)}) custom-call(bf16[6,8,2304]{2,1,0:T(8,128)(2,1)} %bitcast.14, bf16[6,8,2304]{2,1,0:T(8,128)(2,1)} %bitcast.15, f32[1,192]{1,0:T(1,128)} %bitcast.16, ...), custom_call_target="tpu_custom_call" | custom-call | tf_op jit(solution)/shard_map/block/pallas_call | solution.py:536
  51.6 2.1 %results.1 = (bf16[6,8,2304]{2,1,0:T(8,128)(2,1)}, bf16[6,8,2304]{2,1,0:T(8,128)(2,1)}, f32[192,576]{1,0:T(8,128)}, f32[192,192]{1,0:T(8,128)}, f32[192,768]{1,0...) custom-call(bf16[6,8,2304]{2,1,0:T(8,128)(2,1)S(1)} %get-tuple-element.23.m, ...), custom_call_target="tpu_custom_call" | custom-call | tf_op jit(solution)/shard_map/results/pallas_call | solution.py:572

commit v5 on v4

--- a/solution.py
+++ b/solution.py
@@ -34,19 +34,10 @@
                 for r in range(WR):
                     perm[c, r, (2 * w + lev + 1) % 8, w, c, lev, r] = 1
     perm = perm.reshape(TOK, TOK)
-    expand = np.zeros((WC, A, WC, HEADS, A), np.float32)
-    for c in range(WC):
-        for a in range(A):
-            expand[c, a, c, :, a] = 1
-    expand = expand.reshape(TW, HT)
-    head_mask = np.zeros((HEADS, HEAD, WC, HEADS, A), np.float32)
-    for h in range(HEADS):
-        head_mask[h, :, :, h, :] = 1
-    head_mask = head_mask.reshape(C, HT)
-    rep = np.zeros((HEADS, RELP, REL, HEADS, A), np.float32)
+    rep = np.zeros((HEADS, RELP, HEADS, REL, A), np.float32)
     for h in range(HEADS):
         for rel in range(REL):
-            rep[h, rel, rel, h, :] = 1
+            rep[h, rel, h, rel, :] = 1
     rep = np.concatenate([rep.reshape(HEADS * RELP, ZL)] * 3)
     pair = np.zeros((WZ, WZ, WR, WR, WZ, WR, 16), np.float32)
     for lt in range(WZ):
@@ -62,7 +53,7 @@
     level_differs = ((b[:, None] // WR) != (lane_a[None, :] // WR)) & (b[:, None] < A)
     row_differs = ((b[:, None] % WR >= 3) != (lane_a[None, :] % WR >= 3)) & (b[:, None] < A)
     differs = np.stack([level_differs, row_differs]).astype(np.float32)
-    return [np.asarray(v, dtype=BF) for v in (perm, expand, head_mask, rep, pair)] + [entry, differs]
+    return [np.asarray(v, dtype=BF) for v in (perm, rep, pair)] + [entry, differs]
 
 
 def nn(a, b):
@@ -245,7 +236,7 @@
 def block_kernel(
     field_ref, cot_ref, *refs,
 ):
-    count = 14
+    count = 12
     sources, outs, (held, rest) = refs[:count], refs[count:count + 5], (refs[count + 5:2 * count + 5], refs[2 * count + 5:])
     block(field_ref, cot_ref, sources, held, *outs, *rest)
 
@@ -253,13 +244,13 @@
 def block(
     field_ref, cot_ref, sources, held,
     mixed_out, fgrad_out, final0, final1, final_t,
-    x_ref, t_ref, bias_ref, z_ref, p_ref, qblk_ref, q_ref, k_ref, v_ref, kv_ref, ctx_ref, dctx_ref, dproj_ref,
+    x_ref, t_ref, bias_ref, z_ref, p_ref, qblk_ref, dblk_ref, q_ref, k_ref, v_ref, kv_ref, ctx_ref, dctx_ref, dproj_ref, qkv_t, proj_t, fc1_t, fc2_t,
     win_ref, send_ref, grads0, grads1, grads_t, got0, got1, halves0, halves1,
     terms0, terms1, terms_t, part0, part1, part_t, cross0, cross1, cross_t,
     load_sems, local_sems, halo_send, halo_recv, trail_send, trail_recv, core_send, core_recv,
     sum_send, sum_recv, ready,
 ):
-    gain_attn, gain_mlp, qkv_w, proj_w, fc1_w, fc2_w, table, perm, expand, head_mask, rep, pair, entry, differs = held
+    gain_attn, gain_mlp, qkv_w, proj_w, fc1_w, fc2_w, table, perm, rep, pair, entry, differs = held
     lon, lat = lax.axis_index("lon"), lax.axis_index("lat")
     lon_n, lat_n = 32, 4
     west, east = (lon + lon_n - 1) % lon_n, (lon + 1) % lon_n
@@ -286,7 +277,7 @@
     for device in partners:
         pl.semaphore_signal(barrier, inc=1, device_id=device, device_id_type=MESH_ID)
     loads = [pltpu.make_async_copy(a, b, load_sems.at[k]) for k, (a, b) in enumerate(zip(sources, held))]
-    first = (6, 11, 10, 12, 13)
+    first = (6, 9, 8, 10, 11)
     for k in first:
         loads[k].start()
     pl.semaphore_wait(barrier, len(partners))
@@ -342,11 +333,21 @@
             hide = hide + differs[0]
         z = jnp.where(hide > 0.5, MASKED, z)
         for cs in range(WC):
-            bias_ref[w, cs * A:(cs + 1) * A, :] = z[0:A, (11 - cs) * HEADS * A:(11 - cs) * HEADS * A + HT]
+            for h in range(HEADS):
+                at = h * REL * A + (11 - cs) * A
+                bias_ref[w, cs * A:(cs + 1) * A, h * TW:(h + 1) * TW] = z[0:A, at:at + TW]
+
+    qblk_ref[...] = jnp.zeros_like(qblk_ref)
+    dblk_ref[...] = jnp.zeros_like(dblk_ref)
 
     for k in range(len(loads)):
         if k not in first:
             loads[k].wait()
+    qkv_t[...] = qkv_w[...].T
+    proj_t[...] = proj_w[...].T
+    fc1_t[...] = fc1_w[...].T
+    fc2_t[...] = fc2_w[...].T
+
     for copy in halos[0]:
         copy.wait()
     for copy in halos[1]:
@@ -357,25 +358,26 @@
     gain2 = column_of(gain_mlp[...])
     hat1, inv1 = normalise(field)
     normed1 = (hat1 * gain1).astype(BF)
-    projected = tn(qkv_w[...], normed1)
+    projected = nn(qkv_t[...], normed1)
     scaling = HEAD ** (-0.5)
     q_ref[...] = (projected[0:C] * scaling).astype(BF)
     k_ref[...] = projected[C:2 * C].astype(BF)
     v_ref[...] = projected[2 * C:].astype(BF)
     kv_ref[...] = tn(normed1, qkv_w[:, C:]).astype(BF)
-    mask = head_mask[...]
+    blocks = [(slice(h * HEAD, (h + 1) * HEAD), slice(h * TW, (h + 1) * TW)) for h in range(HEADS)]
 
     for w in range(NW):
         rows = slice(w * TW, (w + 1) * TW)
-        qblk = nn(q_ref[:, rows], expand[...]).astype(BF) * mask
-        qblk_ref[w] = qblk
-        scores = nn(kv_ref[rows, 0:C], qblk) + bias_ref[w]
+        for head, cols in blocks:
+            qblk_ref[w, head, cols] = q_ref[head, rows]
+        scores = nn(kv_ref[rows, 0:C], qblk_ref[w]) + bias_ref[w]
         raised = jnp.exp(scores - jnp.max(scores, axis=0, keepdims=True))
         probs = raised * (1.0 / jnp.sum(raised, axis=0, keepdims=True))
         p_ref[w] = probs
-        context = nn(v_ref[:, rows], probs.astype(BF)).astype(BF) * mask
-        ctx_ref[:, rows] = nt(context, expand[...]).astype(BF)
-    attended = tn(proj_w[...], ctx_ref[...]).astype(BF)
+        context = nn(v_ref[:, rows], probs.astype(BF)).astype(BF)
+        for head, cols in blocks:
+            ctx_ref[head, rows] = context[head, cols]
+    attended = nn(proj_t[...], ctx_ref[...]).astype(BF)
 
     for copy in halos[1]:
         copy.wait()
@@ -385,7 +387,7 @@
     resid = field + attended.astype(F32)
     hat2, inv2 = normalise(resid)
     normed2 = (hat2 * gain2).astype(BF)
-    hidden = tn(fc1_w[...], normed2)
+    hidden = nn(fc1_t[...], normed2)
     k0 = 0.7978845608028654
     k1 = 0.044715
     sq = hidden * hidden
@@ -393,7 +395,7 @@
     half = 0.5 * (1.0 + th)
     act = (hidden * half).astype(BF)
     slope = half + 0.5 * hidden * (1.0 - th * th) * (k0 + (3.0 * k0 * k1) * sq)
-    d_act = tn(fc2_w[...], cot_low).astype(BF)
+    d_act = nn(fc2_t[...], cot_low).astype(BF)
     d_pre = (d_act.astype(F32) * slope).astype(BF)
     fc1_grad = nt(normed2, d_pre).astype(BF)
     fc2_grad = nt(cot_low, act).astype(BF)
@@ -418,7 +420,9 @@
             pl.semaphore_wait(ready, len(lines))
             sum0.start()
         rows = slice(w * TW, (w + 1) * TW)
-        dblk = nn(dctx_ref[:, rows], expand[...]).astype(BF) * mask
+        for head, cols in blocks:
+            dblk_ref[w, head, cols] = dctx_ref[head, rows]
+        dblk = dblk_ref[w]
         probs = p_ref[w]
         d_probs = nn(kv_ref[rows, C:], dblk)
         weighted = probs * d_probs
@@ -426,8 +430,9 @@
         d_low = d_scores.astype(BF)
         dproj_ref[2 * C:, rows] = nt(dblk, probs.astype(BF)).astype(BF)
         dproj_ref[C:2 * C, rows] = nt(qblk_ref[w], d_low).astype(BF)
-        d_q = (nn(k_ref[:, rows], d_low) * scaling).astype(BF) * mask
-        dproj_ref[0:C, rows] = nt(d_q, expand[...]).astype(BF)
+        d_q = (nn(k_ref[:, rows], d_low) * scaling).astype(BF)
+        for head, cols in blocks:
+            dproj_ref[head, rows] = d_q[head, cols]
         p_ref[w] = d_scores
 
     dproj = dproj_ref[...]
@@ -444,8 +449,9 @@
     for w in range(NW):
         z_ref[...] = jnp.zeros_like(z_ref)
         for cs in range(WC):
-            at = slice((11 - cs) * HEADS * A, (11 - cs) * HEADS * A + HT)
-            z_ref[0:A, at] += p_ref[w, cs * A:(cs + 1) * A, :]
+            for h in range(HEADS):
+                at = h * REL * A + (11 - cs) * A
+                z_ref[0:A, at:at + TW] += p_ref[w, cs * A:(cs + 1) * A, h * TW:(h + 1) * TW]
         dz = z_ref[...]
         spread = jnp.concatenate([dz * entry[a:a + 1] for a in range(A)], axis=0).astype(BF)
         d_table = nt(nt(rep[0:HEADS * RELP, :], spread).astype(BF), pair[...]).astype(BF)
@@ -460,11 +466,11 @@
     sum_t.start()
 
     d_field = (d_resid + normalise_back(d_win * gain1, hat1, inv1)).astype(BF)
-    fgrad_copies = trail(d_field, 1, fgrad_out)
     sum0.across()
     sum1.across()
+    fgrad_copies = trail(d_field, 1, fgrad_out)
+    sum1.back()
     sum_t.across()
-    sum1.back()
     sum0.back()
     sum_t.back()
     sum1.finish()
@@ -547,11 +553,12 @@
             pltpu.VMEM((NW, TW, HT), F32),
             pltpu.VMEM((16, ZL), F32),
             pltpu.VMEM((NW, TW, HT), F32),
-            pltpu.VMEM((NW, C, HT), BF),
+            pltpu.VMEM((NW, C, HT), BF), pltpu.VMEM((NW, C, HT), BF),
             pltpu.VMEM((C, TOK), BF), pltpu.VMEM((C, TOK), BF), pltpu.VMEM((C, TOK), BF),
             pltpu.VMEM((TOK, 2 * C), BF),
             pltpu.VMEM((C, TOK), BF), pltpu.VMEM((C, TOK), BF),
             pltpu.VMEM((3 * C, TOK), BF),
+            pltpu.VMEM((3 * C, C), BF), pltpu.VMEM((C, C), BF), pltpu.VMEM((HID, C), BF), pltpu.VMEM((HID, C), BF),
             pltpu.VMEM((2,) + tile, BF),
             pltpu.VMEM((2,) + tile, BF),
             pltpu.VMEM((2 * PEERS, ROWS[0], LANES), BF), pltpu.VMEM((2 * PEERS, ROWS[1], LANES), BF), pltpu.VMEM((PEERS, TROWS, LANES), BF),

time: 54 us -> 51.8 us (0.959)
  Pallas kernels: 53.1 us -> 50.8 us
    pallas_call x1, Pallas kernels: 51 us -> 48.7 us  [shards(): pl.pallas_call(block_kernel, out_shape=(sds(tile, BF), sds(tile, BF), sds...]
where the time goes in v5:
time: 51.8 us; the launch traced here: 51.7 us
  Pallas kernels  50.8 us (98%)
  between operations  0.81 us (2%)
    pallas_call x1, Pallas kernels, shards(): pl.pallas_call(block_kernel, out_shape=(sds(tile, BF), sds(tile, BF), sds...  48.7 us
    pallas_call x1, Pallas kernels, shards(): pl.pallas_call(results_kernel, out_shape=[sds(tile, BF)] * 2 + [sds(v, F3...  2.13 us

profile of v5, /device:TPU:1, one launch (start us, length us, event | category | flops | bytes accessed | tf_op | source)
XLA Modules:
  0.0 51.7 jit_solution(8306272023382829282)
XLA Ops:
  0.6 48.7 %block.1 = (bf16[6,8,2304]{2,1,0:T(8,128)(2,1)S(1)}, bf16[6,8,2304]{2,1,0:T(8,128)(2,1)S(1)}, bf16[32,80,128]{2,1,0:T(8,128)(2,1)S(1)}, bf16[32,32,128]{2,1,0:T(8,128)(2,1)S(1)}, bf16[16,48,128]{2,1,0:T(8,128)(2,1)S(1)}) custom-call(bf16[6,8,2304]{2,1,0:T(8,128)(2,1)} %bitcast.14, bf16[6,8,2304]{2,1,0:T(8,128)(2,1)} %bitcast.15, f32[1,192]{1,0:T(1,128)} %bitcast.16, ...), custom_call_target="tpu_custom_call" | custom-call | tf_op jit(solution)/shard_map/block/pallas_call | solution.py:542
  49.4 2.1 %results.1 = (bf16[6,8,2304]{2,1,0:T(8,128)(2,1)}, bf16[6,8,2304]{2,1,0:T(8,128)(2,1)}, f32[192,576]{1,0:T(8,128)}, f32[192,192]{1,0:T(8,128)}, f32[192,768]{1,0...) custom-call(bf16[6,8,2304]{2,1,0:T(8,128)(2,1)S(1)} %get-tuple-element.23.m, ...), custom_call_target="tpu_custom_call" | custom-call | tf_op jit(solution)/shard_map/results/pallas_call | solution.py:579

commit v6 on v5

--- a/solution.py
+++ b/solution.py
@@ -102,6 +102,7 @@
 ROWS = (80, 32)
 TROWS = 48
 MESH_ID = pl.DeviceIdType.MESH
+FARTHEST_FIRST = sorted(range(1, PEERS), key=lambda s: -sum(min(far, 4 - far) for far in divmod(s, 4)))
 
 
 def place():
@@ -143,10 +144,10 @@
         self.few = cross.at[pl.ds(1, self.count - 1)]
 
     def in_plane(self, s):
-        p = (self.me + s) % PEERS
         at = list(self.at)
-        at[self.axes[0]], at[self.axes[1]] = p // 4, p % 4
-        return p, device_at(*at)
+        for axis, far in zip(self.axes, divmod(s, 4)):
+            at[axis] = (at[axis] + far) % 4
+        return at[self.axes[0]] * 4 + at[self.axes[1]], device_at(*at)
 
     def along(self, s):
         at = list(self.at)
@@ -154,7 +155,7 @@
         return device_at(*at)
 
     def start(self):
-        for s in range(1, PEERS):
+        for s in FARTHEST_FIRST:
             p, device = self.in_plane(s)
             remote(self.piece(p), self.terms.at[s], self.sends.at[0], self.recvs.at[0], device).start()
 
@@ -172,7 +173,7 @@
         value = total(self.cross, self.count)
         self.part[1] = value
         self.final[self.first + self.me] = value
-        for s in range(1, PEERS):
+        for s in FARTHEST_FIRST:
             remote(self.part.at[1], self.final.at[self.first + self.me], self.sends.at[2], self.recvs.at[2], self.in_plane(s)[1]).start()
 
     def finish(self):
@@ -257,7 +258,7 @@
     above, below = (lat + lat_n - 1) % lat_n, (lat + 1) % lat_n
 
     sum0, sum1 = [
-        CoreSum((0, 1, 2), grads, got, halves, final, (core_send.at[k], core_recv.at[k]), terms, part, cross, sum_send.at[k], sum_recv.at[k])
+        CoreSum((0, 1, 2) if k == 0 else (0, 2, 1), grads, got, halves, final, (core_send.at[k], core_recv.at[k]), terms, part, cross, sum_send.at[k], sum_recv.at[k])
         for k, (grads, got, halves, final, terms, part, cross) in enumerate((
             (grads0, got0, halves0, final0, terms0, part0, cross0), (grads1, got1, halves1, final1, terms1, part1, cross1),
         ))
@@ -469,8 +470,8 @@
     sum0.across()
     sum1.across()
     fgrad_copies = trail(d_field, 1, fgrad_out)
+    sum_t.across()
     sum1.back()
-    sum_t.across()
     sum0.back()
     sum_t.back()
     sum1.finish()

time: 51.8 us -> 50.6 us (0.977)
  Pallas kernels: 50.8 us -> 49.7 us
    pallas_call x1, Pallas kernels: 48.7 us -> 47.6 us  [shards(): pl.pallas_call(block_kernel, out_shape=(sds(tile, BF), sds(tile, BF), sds...]
where the time goes in v6:
time: 50.6 us; the launch traced here: 50.5 us
  Pallas kernels  49.7 us (98%)
  between operations  0.81 us (2%)
    pallas_call x1, Pallas kernels, shards(): pl.pallas_call(block_kernel, out_shape=(sds(tile, BF), sds(tile, BF), sds...  47.6 us
    pallas_call x1, Pallas kernels, shards(): pl.pallas_call(results_kernel, out_shape=[sds(tile, BF)] * 2 + [sds(v, F3...  2.13 us

profile of v6, /device:TPU:1, one launch (start us, length us, event | category | flops | bytes accessed | tf_op | source)
XLA Modules:
  0.0 50.5 jit_solution(1762304226560101917)
XLA Ops:
  0.6 47.6 %block.1 = (bf16[6,8,2304]{2,1,0:T(8,128)(2,1)S(1)}, bf16[6,8,2304]{2,1,0:T(8,128)(2,1)S(1)}, bf16[32,80,128]{2,1,0:T(8,128)(2,1)S(1)}, bf16[32,32,128]{2,1,0:T(8,128)(2,1)S(1)}, bf16[16,48,128]{2,1,0:T(8,128)(2,1)S(1)}) custom-call(bf16[6,8,2304]{2,1,0:T(8,128)(2,1)} %bitcast.14, bf16[6,8,2304]{2,1,0:T(8,128)(2,1)} %bitcast.15, f32[1,192]{1,0:T(1,128)} %bitcast.16, ...), custom_call_target="tpu_custom_call" | custom-call | tf_op jit(solution)/shard_map/block/pallas_call | solution.py:543
  48.2 2.1 %results.1 = (bf16[6,8,2304]{2,1,0:T(8,128)(2,1)}, bf16[6,8,2304]{2,1,0:T(8,128)(2,1)}, f32[192,576]{1,0:T(8,128)}, f32[192,192]{1,0:T(8,128)}, f32[192,768]{1,0...) custom-call(bf16[6,8,2304]{2,1,0:T(8,128)(2,1)S(1)} %get-tuple-element.23.m, ...), custom_call_target="tpu_custom_call" | custom-call | tf_op jit(solution)/shard_map/results/pallas_call | solution.py:580
